TPU v7x, 32 devices: a whole 2x2x4 slice. The times are simulated.
32 devices in a mesh: seq: 16 (over z, x, core), head: 2 (over y).
Axes of the slice: x: 2, y: 2, z: 4, core: 2. Of those that a mesh axis runs over, the one named last changes fastest.
Arguments:
- normed: bfloat16 [8192, 5376], P('seq'), may hold values from -6 to 6
- cotangent: bfloat16 [8192, 2048], P('seq', 'head'), may hold values from -6 to 6
- qkv_master: float32 [5376, 8, 512], P('seq', 'head'), may hold values from -0.078125 to 0.078125
- adam_first: float32 [5376, 8, 512], P('seq', 'head'), may hold values from -6 to 6
- adam_second: float32 [5376, 8, 512], P('seq', 'head'), may hold values from 0.5 to 20
- skip_flag: int32 [8], replicated, may hold values 0 or 1
- scale_exponent: int32 [1], replicated, may hold values from 4 to 8
Outputs:
- attn_out: bfloat16 [8192, 2048], P('seq', 'head')
- d_tokens: bfloat16 [8192, 5376], P(('seq', 'head'))
- new_master: float32 [5376, 8, 512], P('seq', 'head')
- new_first: float32 [5376, 8, 512], P('seq', 'head')
- new_second: float32 [5376, 8, 512], P('seq', 'head')
All inputs are finite; a program needn't handle non-finite values.
Results may differ from a plain program's by a relative error of at most 0.0095.
Values may be sent and summed in bfloat16 or wider, within the bound.
A program may use at most 256 MiB of HBM per device.

v0:
```python
import jax
import jax.numpy as jnp
from jax import lax
from jax.sharding import PartitionSpec as P

HEAD_DIM = 128
ATTEND_SPAN = 1024
ATTN_SCALAR = 168
Q_PER_KV = 2
ADAM_STEP = 1000


norm_eps = 1e-06
beta_one = 0.9
beta_two = 0.95
adam_eps = 1e-08
learn_rate = 0.01
weight_decay = 0.1


def shifted(block, axis, distance):
    devices = range(lax.axis_size(axis))
    route = [(i - distance, i) for i in devices if i - distance in devices]
    return lax.ppermute(block, axis, route)


def head_norm(raw_vals):
    factor = lax.rsqrt(jnp.mean(raw_vals * raw_vals, axis=-1, keepdims=True) + norm_eps)
    return (raw_vals * factor, factor)


def norm_back(raw_vals, factor, grad_in):
    inner_mean = jnp.mean(raw_vals * grad_in, axis=-1, keepdims=True)
    return factor * grad_in - raw_vals * factor * factor * factor * inner_mean


def window_kernel(query_tile, key_tile, query_start, key_start):
    score_scale = float(ATTN_SCALAR) ** (-0.5)
    scores = (
        jnp.einsum("tgqd,lgd->gqtl", query_tile, key_tile, preferred_element_type=jnp.float32)
        * score_scale
    )
    query_pos = query_start + jnp.arange(query_tile.shape[0], dtype=jnp.int32)
    key_pos = key_start + jnp.arange(key_tile.shape[0], dtype=jnp.int32)
    gap_len = query_pos[:, None] - key_pos[None, :]
    allowed = (key_pos[None, :] >= 0) & (gap_len >= 0) & (gap_len < ATTEND_SPAN)
    return jnp.where(allowed, jnp.exp(scores), 0.0)


def per_device(normed, cotangent, qkv_master, adam_first, adam_second, skip_flag, scale_exponent):
    tok_rows = normed.shape[0]
    model_width = normed.shape[1]
    own_rows = qkv_master.shape[0]
    kv_groups = qkv_master.shape[1]
    col_count = qkv_master.shape[2]
    q_cols = Q_PER_KV * HEAD_DIM
    halo_span = ATTEND_SPAN // tok_rows
    score_scale = float(ATTN_SCALAR) ** (-0.5)
    seq_pos = lax.axis_index("seq")
    master16 = qkv_master.astype(jnp.bfloat16)
    full16 = lax.all_gather(master16, "seq", axis=0, tiled=True).reshape(
        model_width, kv_groups * col_count
    )
    qkv = jnp.dot(normed, full16, preferred_element_type=jnp.float32).reshape(
        tok_rows, kv_groups, col_count
    )
    q_raw = qkv[:, :, :q_cols].reshape(tok_rows, kv_groups, Q_PER_KV, HEAD_DIM)
    k_raw = qkv[:, :, q_cols : q_cols + HEAD_DIM]
    v_raw = qkv[:, :, q_cols + HEAD_DIM :]
    q_unit, q_factor = head_norm(q_raw)
    k_unit, k_factor = head_norm(k_raw)
    queries = q_unit.astype(jnp.bfloat16)
    key_tiles = k_unit.astype(jnp.bfloat16)
    values = v_raw.astype(jnp.bfloat16)
    key_list = [key_tiles]
    value_list = [values]
    for shift_step in range(1, halo_span + 1):
        far_keys, far_values = shifted((key_tiles, values), "seq", shift_step)
        key_list.insert(0, far_keys)
        value_list.insert(0, far_values)
    ext_keys = jnp.concatenate(key_list, 0)
    ext_values = jnp.concatenate(value_list, 0)
    query_start = seq_pos * tok_rows
    key_start = query_start - halo_span * tok_rows
    kernel = window_kernel(queries, ext_keys, query_start, key_start)
    totals = jnp.sum(kernel, axis=-1, keepdims=True)
    prob_tile = (kernel / totals).astype(jnp.bfloat16)
    attention_blend = jnp.einsum(
        "gqtl,lgd->tgqd", prob_tile, ext_values, preferred_element_type=jnp.float32
    )
    attn_out = attention_blend.astype(jnp.bfloat16).reshape(tok_rows, kv_groups * q_cols)
    scale_power = jnp.left_shift(jnp.int32(1), scale_exponent[0]).astype(jnp.float32)
    grad_out = (cotangent.astype(jnp.float32) * scale_power).astype(jnp.bfloat16)
    grad_out = grad_out.reshape(tok_rows, kv_groups, Q_PER_KV, HEAD_DIM)
    row_delta = jnp.transpose(
        jnp.sum(grad_out.astype(jnp.float32) * attention_blend, axis=-1), (1, 2, 0)
    )
    grad_probs = jnp.einsum(
        "tgqd,lgd->gqtl", grad_out, ext_values, preferred_element_type=jnp.float32
    )
    grad_scores = (
        prob_tile.astype(jnp.float32) * (grad_probs - row_delta[..., None]) * score_scale
    ).astype(jnp.bfloat16)
    grad_queries = jnp.einsum(
        "gqtl,lgd->tgqd", grad_scores, ext_keys, preferred_element_type=jnp.float32
    )
    grad_keys_ext = jnp.einsum(
        "gqtl,tgqd->lgd", grad_scores, queries, preferred_element_type=jnp.float32
    )
    grad_values_ext = jnp.einsum(
        "gqtl,tgqd->lgd", prob_tile, grad_out, preferred_element_type=jnp.float32
    )
    own_start = halo_span * tok_rows
    grad_keys = grad_keys_ext[own_start:]
    gradient_value_rows = grad_values_ext[own_start:]
    for shift_step in range(1, halo_span + 1):
        block_low = (halo_span - shift_step) * tok_rows
        back_keys, back_values = shifted(
            (
                grad_keys_ext[block_low : block_low + tok_rows],
                grad_values_ext[block_low : block_low + tok_rows],
            ),
            "seq",
            -shift_step,
        )
        grad_keys = grad_keys + back_keys
        gradient_value_rows = gradient_value_rows + back_values
    grad_qraw = norm_back(q_raw, q_factor, grad_queries)
    grad_kraw = norm_back(k_raw, k_factor, grad_keys)
    grad_qkv = jnp.concatenate(
        [grad_qraw.reshape(tok_rows, kv_groups, q_cols), grad_kraw, gradient_value_rows], -1
    )
    grad_qkv = grad_qkv.astype(jnp.bfloat16).reshape(tok_rows, kv_groups * col_count)
    row_part = grad_qkv
    d_tokens = lax.psum_scatter(
        lax.dot_general(
            row_part, full16, (((1,), (1,)), ((), ())), preferred_element_type=jnp.float32
        ),
        "head",
        scatter_dimension=0,
        tiled=True,
    ).astype(jnp.bfloat16)
    row_part = normed
    whole_term = lax.dot_general(
        row_part, grad_qkv, (((0,), (0,)), ((), ())), preferred_element_type=jnp.float32
    ).reshape(lax.axis_size("seq"), own_rows, kv_groups * col_count)
    received = lax.all_to_all(whole_term, "seq", split_axis=0, concat_axis=0, tiled=True)
    summed = jnp.sum(received, axis=0)
    gradient = (summed / scale_power).reshape(own_rows, kv_groups, col_count)
    first_new = beta_one * adam_first + (1.0 - beta_one) * gradient
    second_new = beta_two * adam_second + (1.0 - beta_two) * gradient * gradient
    first_fix = 1.0 - beta_one**ADAM_STEP
    second_fix = 1.0 - beta_two**ADAM_STEP
    update = first_new / first_fix / (jnp.sqrt(second_new / second_fix) + adam_eps)
    master_new = qkv_master - learn_rate * (update + weight_decay * qkv_master)
    own_flags = lax.dynamic_slice_in_dim(
        skip_flag, lax.axis_index("head") * kv_groups, kv_groups, 0
    )
    applied = (own_flags == 0)[None, :, None]
    return (
        attn_out,
        d_tokens,
        jnp.where(applied, master_new, qkv_master),
        jnp.where(applied, first_new, adam_first),
        jnp.where(applied, second_new, adam_second),
    )


def solution(mesh):
    return jax.shard_map(
        per_device,
        mesh=mesh,
        in_specs=(
            P("seq", None),
            P("seq", "head"),
            P("seq", "head", None),
            P("seq", "head", None),
            P("seq", "head", None),
            P(),
            P(),
        ),
        out_specs=(
            P("seq", "head"),
            P(("seq", "head"), None),
            P("seq", "head", None),
            P("seq", "head", None),
            P("seq", "head", None),
        ),
        check_vma=False,
    )
```

profile of v0, /device:TPU:8, one launch (start us, length us, event | category | flops | bytes accessed | tf_op | source)
XLA Modules:
  0.0 1371.0 jit_solution(4987565901995469820)
XLA Ops:
  7.2 3.6 copy.60
  12.8 113.1 %all-gather.2.cloned.1.call-done = bf16[5376,4,512]{2,0,1:T(8,128)(2,1)} async-done(((bf16[336,4,512]{2,0,1:T(8,128)(2,1)}), bf16[5376,4,512]{2,0,1:T(8,128)(2,1)}) %all-gather.2.cloned.1.call-update) | async-done | bytes 22020112 | tf_op jit(solution)/shard_map/all_gather | solution.py:61
  125.9 26.8 %copy.27 = bf16[5376,4,512]{0,2,1:T(8,128)(2,1)} copy(bf16[5376,4,512]{2,0,1:T(8,128)(2,1)} %all-gather.2.cloned.1.call-done) | data formatting | bytes 44040192 | tf_op jit(solution)/shard_map/all_gather | solution.py:61
  152.7 16.4 %fusion.3 = f32[512,4,512]{0,2,1:T(8,128)S(1)} fusion(bf16[5376,4,512]{0,2,1:T(8,128)(2,1)} %copy.27, bf16[512,5376]{1,0:T(8,128)(2,1)} %param.7), kind=kOutput, calls=%fused_computation.7 | convolution fusion | flops 11274289152 | bytes 31719424 | tf_op jit(solution)/shard_map/dot_general | solution.py:64
  191.0 13.5 fusion.5
  204.6 11.0 divide_convert_fusion
  215.6 7.8 convolution_bitcast_fusion.2
  226.4 7.7 collective-permute-start.6
  236.4 4.1 bitcast_convert_fusion
  241.8 10.4 fusion.2
  252.2 8.7 convolution_bitcast_fusion.3
  266.6 5.7 fusion.11
  281.2 10.5 collective-permute-done.4
  291.7 13.4 collective-permute-done.5
  307.4 3.2 multiply_subtract_fusion
  315.9 22.7 %convolution_bitcast_fusion = f32[5376,2048]{0,1:T(8,128)} fusion(bf16[512,2048]{0,1:T(8,128)(2,1)} %bitcast.105, bf16[512,5376]{1,0:T(8,128)(2,1)} %param.7), kind=kOutput, calls=%fused_computation | convolution fusion | flops 11274289152 | bytes 51642368 | tf_op jit(solution)/shard_map/dot_general | solution.py:144
  338.6 42.8 %copy.41 = f32[5376,2048]{1,0:T(8,128)} copy(f32[5376,2048]{0,1:T(8,128)} %convolution_bitcast_fusion) | data formatting | bytes 88080384 | tf_op jit(solution)/shard_map/dot_general | solution.py:144
  381.4 6.4 all-to-all-start
  388.1 18.9 %convolution_bitcast_fusion.1 = f32[512,5376]{1,0:T(8,128)} fusion(bf16[5376,4,512]{2,0,1:T(8,128)(2,1)} %all-gather.2.cloned.1.call-done, bf16[512,4,128]{2,0,1:T(8,128)(2,1)S(1)} %copy-done.8, bf16[512,4,128]{2,0,1:T(8,128)(2,1)S(1)} %copy.38, bf16[512,4,256]{2,0,1:T(8,128)(2,1)S(1)} %copy-done.6), kind=kOutput, calls=%fused_computation.10 | convolution fusion | flops 11280580608 | bytes 35127296 | tf_op jit(solution)/shard_map/dot_general | solution.py:136
  409.5 125.2 %reduce-scatter.2.cloned.1.call-done = f32[256,5376]{1,0:T(8,128)} async-done(((f32[512,5376]{1,0:T(8,128)}), f32[256,5376]{1,0:T(8,128)}) %reduce-scatter.2.cloned.1.call-update) | async-done | bytes 5505040 | tf_op jit(solution)/shard_map/reduce_scatter | solution.py:135
  534.7 4.4 convert_element_type.60
  539.1 792.3 %all-to-all-done = f32[16,336,2048]{2,1,0:T(8,128)} async-done(((f32[16,336,2048]{2,1,0:T(8,128)}), f32[16,336,2048]{2,1,0:T(8,128)}, u32[]{:S(2)}, u32[]{:S(2)}) %all-to-all-start) | async-done | bytes 44040224 | tf_op jit(solution)/shard_map/all_to_all | solution.py:147
  1331.4 17.8 %reduce_sum.69 = f32[336,2048]{1,0:T(8,128)} reduce(f32[16,336,2048]{2,1,0:T(8,128)} %all-to-all-done, f32[]{:T(128)} %constant.25.clone.1), dimensions={0}, to_apply=%region_7.8 | reduce | flops 10321920 | bytes 46792708 | tf_op jit(solution)/shard_map/reduce_sum | solution.py:148
  1354.1 9.6 fusion.14
  (80 shorter events, 59.6 us)
Async XLA Ops:
  7.2 118.7 %all-gather.2.cloned.1.call-start = ((), (), s32[]{:S(2)}) async-start(), calls=%async_computation.2 | async-start | bytes 23396352 | tf_op jit(solution)/shard_map/all_gather | solution.py:61
  12.8 178.2 %copy-start.7 = (pred[512,1536]{0,1:T(8,128)(4,1)}, pred[512,1536]{0,1:T(8,128)(4,1)S(1)}, u32[]{:S(2)}) copy-start(pred[512,1536]{0,1:T(8,128)(4,1)S(1)} %fusion.8) | copy-start | bytes 2359300
  169.1 7.5 copy-start.11
  171.2 19.8 %copy-start.9 = (bf16[512,4,128]{0,2,1:T(8,128)(2,1)}, bf16[512,4,128]{0,2,1:T(8,128)(2,1)S(1)}, u32[]{:S(2)}) copy-start(bf16[512,4,128]{0,2,1:T(8,128)(2,1)S(1)} %multiply_convert_fusion.2) | copy-start | bytes 1572868
  171.2 17.3 %collective-permute-start.3 = (bf16[512,4,128]{0,2,1:T(8,128)(2,1)S(1)}, bf16[512,4,128]{0,2,1:T(8,128)(2,1)S(1)}, u32[]{:S(2)}, u32[]{:S(2)}) collective-permute-start(bf16[512,4,128]{0,2,1:T(8,128)(2,1)S(1)} %multiply_convert_fusion.2), channel_id=1, source_target_pairs={{0,2},{2,4},{4,6},{6,8},{8,10},{10,12},{12,14},{14,16},{16,18},{18... | collective-permute-start | bytes 1572872 | tf_op jit(solution)/shard_map/ppermute | solution.py:24
  173.4 17.7 %collective-permute-start.2 = (bf16[512,4,128]{0,2,1:T(8,128)(2,1)S(1)}, bf16[512,4,128]{0,2,1:T(8,128)(2,1)S(1)}, u32[]{:S(2)}, u32[]{:S(2)}) collective-permute-start(bf16[512,4,128]{0,2,1:T(8,128)(2,1)S(1)} %multiply_convert_fusion.2), channel_id=1, source_target_pairs={{0,4},{2,6},{4,8},{6,10},{8,12},{10,14},{12,16},{14,18},{16,20},{1... | collective-permute-start | bytes 1572872 | tf_op jit(solution)/shard_map/ppermute | solution.py:24
  180.2 56.2 %collective-permute-start.1 = (bf16[512,4,128]{0,2,1:T(8,128)(2,1)}, bf16[512,4,128]{0,2,1:T(8,128)(2,1)}, u32[]{:S(2)}, u32[]{:S(2)}) collective-permute-start(bf16[512,4,128]{0,2,1:T(8,128)(2,1)} %slice.67), channel_id=1, source_target_pairs={{0,2},{2,4},{4,6},{6,8},{8,10},{10,12},{12,14},{14,16},{16,18},{18... | collective-permute-start | bytes 1572872 | tf_op jit(solution)/shard_map/ppermute | solution.py:24
  183.4 53.0 %collective-permute-start = (bf16[512,4,128]{0,2,1:T(8,128)(2,1)}, bf16[512,4,128]{0,2,1:T(8,128)(2,1)}, u32[]{:S(2)}, u32[]{:S(2)}) collective-permute-start(bf16[512,4,128]{0,2,1:T(8,128)(2,1)} %slice.67), channel_id=1, source_target_pairs={{0,4},{2,6},{4,8},{6,10},{8,12},{10,14},{12,16},{14,18},{16,20},{1... | collective-permute-start | bytes 1572872 | tf_op jit(solution)/shard_map/ppermute | solution.py:24
  188.5 16.1 %copy-start.12 = (bf16[512,4,128]{0,2,1:T(8,128)(2,1)}, bf16[512,4,128]{0,2,1:T(8,128)(2,1)S(1)}, u32[]{:S(2)}) copy-start(bf16[512,4,128]{0,2,1:T(8,128)(2,1)S(1)} %collective-permute-done.3) | copy-start | bytes 1572868
  191.0 13.5 copy-start.14
  215.6 20.8 %copy-start = (bf16[4,2,512,1536]{2,3,1,0:T(8,128)(2,1)}, bf16[4,2,512,1536]{2,3,1,0:T(8,128)(2,1)S(1)}, u32[]{:S(2)}) copy-start(bf16[4,2,512,1536]{2,3,1,0:T(8,128)(2,1)S(1)} %divide_convert_fusion) | copy-start | bytes 37748740
  226.4 49.8 %collective-permute-start.6 = (f32[512,4,128]{0,2,1:T(8,128)}, f32[512,4,128]{0,2,1:T(8,128)}, u32[]{:S(2)}, u32[]{:S(2)}) collective-permute-start(f32[512,4,128]{0,2,1:T(8,128)} %get-tuple-element.20), channel_id=1, source_target_pairs={{2,0},{4,2},{6,4},{8,6},{10,8},{12,10},{14,12},{16,14},{18,16},{20... | collective-permute-start | bytes 3145736 | tf_op jit(solution)/shard_map/ppermute | solution.py:24
  234.1 6.4 copy-start.3
  234.1 42.1 %collective-permute-start.7 = (f32[512,4,128]{0,2,1:T(8,128)}, f32[512,4,128]{0,2,1:T(8,128)}, u32[]{:S(2)}, u32[]{:S(2)}) collective-permute-start(f32[512,4,128]{0,2,1:T(8,128)} %get-tuple-element.21), channel_id=1, source_target_pairs={{4,0},{6,2},{8,4},{10,6},{12,8},{14,10},{16,12},{18,14},{20,16},{2... | collective-permute-start | bytes 3145736 | tf_op jit(solution)/shard_map/ppermute | solution.py:24
  241.8 10.4 copy-start.2
  260.9 5.7 copy-start.10
  260.9 5.7 copy-start.13
  260.9 5.7 copy-start.15
  262.5 29.2 %collective-permute-start.4 = (f32[512,4,128]{0,2,1:T(8,128)}, f32[512,4,128]{0,2,1:T(8,128)}, u32[]{:S(2)}, u32[]{:S(2)}) collective-permute-start(f32[512,4,128]{0,2,1:T(8,128)} %get-tuple-element.18), channel_id=1, source_target_pairs={{2,0},{4,2},{6,4},{8,6},{10,8},{12,10},{14,12},{16,14},{18,16},{20... | collective-permute-start | bytes 3145736 | tf_op jit(solution)/shard_map/ppermute | solution.py:24
  264.4 40.6 %collective-permute-start.5 = (f32[512,4,128]{0,2,1:T(8,128)}, f32[512,4,128]{0,2,1:T(8,128)}, u32[]{:S(2)}, u32[]{:S(2)}) collective-permute-start(f32[512,4,128]{0,2,1:T(8,128)} %get-tuple-element.19), channel_id=1, source_target_pairs={{4,0},{6,2},{8,4},{10,6},{12,8},{14,10},{16,12},{18,14},{20,16},{2... | collective-permute-start | bytes 3145736 | tf_op jit(solution)/shard_map/ppermute | solution.py:24
  381.4 6.7 copy-start.6
  381.4 6.7 copy-start.8
  381.4 950.0 %all-to-all-start = ((f32[16,336,2048]{2,1,0:T(8,128)}), f32[16,336,2048]{2,1,0:T(8,128)}, u32[]{:S(2)}, u32[]{:S(2)}) async-start(f32[16,336,2048]{2,1,0:T(8,128)} %bitcast.100), calls=%async_computation.1 | async-start | bytes 88080384 | tf_op jit(solution)/shard_map/all_to_all | solution.py:147
  387.8 147.0 %reduce-scatter.2.cloned.1.call-start = ((), (), s32[]{:S(2)}) async-start(), calls=%async_computation.3 | async-start | bytes 16515072 | tf_op jit(solution)/shard_map/reduce_scatter | solution.py:135
  (4 other events, 5.1 us)
Sparse Core Ops, SparseCore 0:
  11.0 114.8 all-gather.1
  407.1 127.5 reduce-scatter.1
where the time goes:
time: 1380 us; the launch traced here: 1370 us
  waiting for transfers between devices  1060 us (77%)
  matrix products  108 us (8%)
  local copies, waits for them, and re-layouts  97.3 us (7%)
  other arithmetic  60.5 us (4%)
  starting transfers between devices  32.3 us (2%)
  between operations  15.5 us (1%)
    all_to_all x1, waiting for transfers between devices, per_device(): lax.all_to_all(whole_term, 'seq', split_axis=0, concat_axis=0, tiled=True)  792 us
    reduce_scatter x1, waiting for transfers between devices, per_device(): lax.psum_scatter(lax.dot_general(row_part, full16, (((1,), (1,)), ((), ()...  125 us
    all_gather x1, waiting for transfers between devices, per_device(): lax.all_gather(master16, 'seq', axis=0, tiled=True)  113 us
    dot_general x1, local copies, waits for them, and re-layouts, per_device(): lax.dot_general(row_part, grad_qkv, (((0,), (0,)), ((), ())), preferred_e...  42.8 us
  transfers between devices with their start and end apart: 11, of which 6 were waited for; matrix products, arithmetic and copies ran while one was open for 8% of the time, Pallas kernels for 0%

commit v1 on v0

v1 whole, which is shorter than its diff:
```python
import functools

import jax
import jax.numpy as jnp
from jax import lax
from jax.experimental import pallas as pl
from jax.experimental.pallas import tpu as pltpu
from jax.sharding import PartitionSpec as P

HEAD_DIM = 128
ATTEND_SPAN = 1024
ATTN_SCALAR = 168
Q_PER_KV = 2
ADAM_STEP = 1000
TILE = 128


norm_eps = 1e-06
beta_one = 0.9
beta_two = 0.95
adam_eps = 1e-08
learn_rate = 0.01
weight_decay = 0.1
score_scale = float(ATTN_SCALAR) ** (-0.5)
log2_e = 1.4426950408889634


def shifted(block, axis, distance):
    devices = range(lax.axis_size(axis))
    route = [(i - distance, i) for i in devices if i - distance in devices]
    return lax.ppermute(block, axis, route)


def head_norm(raw_vals):
    factor = lax.rsqrt(jnp.mean(raw_vals * raw_vals, axis=-1, keepdims=True) + norm_eps)
    return (raw_vals * factor, factor)


def norm_back(raw_vals, factor, grad_in):
    inner_mean = jnp.mean(raw_vals * grad_in, axis=-1, keepdims=True)
    return factor * grad_in - raw_vals * factor * factor * factor * inner_mean


def dot_nt(a, b):
    return lax.dot_general(a, b, (((1,), (1,)), ((), ())), preferred_element_type=jnp.float32)


def dot_nn(a, b):
    return jnp.dot(a, b, preferred_element_type=jnp.float32)


def attention_kernel(halo_span, start_ref, qkv_ref, *refs):
    kv_refs = refs[: halo_span + 1]
    go_ref, out_ref, gq_ref, own_ref = refs[halo_span + 1 : halo_span + 5]
    back_refs = refs[halo_span + 5 : 2 * halo_span + 5]
    kv, kv_t, acc, e_buf = refs[2 * halo_span + 5 :]
    rows = qkv_ref.shape[0]
    d = HEAD_DIM
    for n, ref in enumerate(kv_refs):
        block = ref[...]
        kv[n * rows : (n + 1) * rows, :] = block
        kv_t[:, n * rows : (n + 1) * rows] = jnp.transpose(block.astype(jnp.float32)).astype(
            jnp.bfloat16
        )
    acc[...] = jnp.zeros_like(acc)
    chunks = ATTEND_SPAN // TILE + 1
    heads = Q_PER_KV
    for t in range(rows // TILE):
        r0 = t * TILE
        q_raw = jnp.concatenate(
            [qkv_ref[r0 : r0 + TILE, h * d : (h + 1) * d] for h in range(heads)], 0
        )
        q_unit, q_factor = head_norm(q_raw)
        q16 = q_unit.astype(jnp.bfloat16)
        go = jnp.concatenate([go_ref[r0 : r0 + TILE, h * d : (h + 1) * d] for h in range(heads)], 0)
        key_row = lax.broadcasted_iota(jnp.int32, (TILE, heads * TILE), 0)
        query_col = lax.broadcasted_iota(jnp.int32, (TILE, heads * TILE), 1) % TILE
        total = jnp.zeros((1, heads * TILE), jnp.float32)
        for c in range(chunks):
            k0 = r0 + c * TILE
            scores = dot_nt(kv[k0 : k0 + TILE, :d], q16)
            e = jnp.exp2(scores * (score_scale * log2_e))
            if c == 0:
                e = jnp.where(key_row > query_col, e, 0.0)
            if c == chunks - 1:
                e = jnp.where(key_row <= query_col, e, 0.0)
            if k0 < ATTEND_SPAN:
                e = e * jnp.where(start_ref[0] + k0 >= 0, 1.0, 0.0)
            total = total + jnp.sum(e, axis=0, keepdims=True)
            e_buf[c * TILE : (c + 1) * TILE, :] = e
        inverse = 1.0 / total
        mixed_t = jnp.zeros((d, heads * TILE), jnp.float32)
        for c in range(chunks):
            k0 = r0 + c * TILE
            p = e_buf[c * TILE : (c + 1) * TILE, :] * inverse
            e_buf[c * TILE : (c + 1) * TILE, :] = p
            mixed_t = mixed_t + dot_nn(kv_t[d:, k0 : k0 + TILE], p.astype(jnp.bfloat16))
        go_t = jnp.transpose(go.astype(jnp.float32))
        delta = jnp.sum(go_t * mixed_t, axis=0, keepdims=True)
        mixed = jnp.transpose(mixed_t).astype(jnp.bfloat16)
        for h in range(heads):
            out_ref[r0 : r0 + TILE, h * d : (h + 1) * d] = mixed[h * TILE : (h + 1) * TILE]
        gq_t = jnp.zeros((d, heads * TILE), jnp.float32)
        for c in range(chunks):
            k0 = r0 + c * TILE
            p = e_buf[c * TILE : (c + 1) * TILE, :]
            grad_p = dot_nt(kv[k0 : k0 + TILE, d:], go)
            grad_s = (p * (grad_p - delta)).astype(jnp.bfloat16)
            gq_t = gq_t + dot_nn(kv_t[:d, k0 : k0 + TILE], grad_s)
            acc[k0 : k0 + TILE, :d] += dot_nn(grad_s, q16)
            acc[k0 : k0 + TILE, d:] += dot_nn(p.astype(jnp.bfloat16), go)
        gq = jnp.transpose(gq_t) * score_scale
        gq_raw = norm_back(q_raw, q_factor, gq).astype(jnp.bfloat16)
        for h in range(heads):
            gq_ref[r0 : r0 + TILE, h * d : (h + 1) * d] = gq_raw[h * TILE : (h + 1) * TILE]
    own0 = halo_span * rows
    own_ref[:, :d] = acc[own0:, :d] * score_scale
    own_ref[:, d:] = acc[own0:, d:]
    for n, ref in enumerate(back_refs):
        low = (halo_span - 1 - n) * rows
        ref[:, :d] = (acc[low : low + rows, :d] * score_scale).astype(jnp.bfloat16)
        ref[:, d:] = acc[low : low + rows, d:].astype(jnp.bfloat16)


def group_attention(qkv, kv_list, grad_out, key_start):
    rows = qkv.shape[0]
    halo_span = len(kv_list) - 1
    d = HEAD_DIM
    q_cols = Q_PER_KV * d
    ext = (halo_span + 1) * rows
    window = ATTEND_SPAN + TILE
    elems = Q_PER_KV * rows * window
    vmem = pl.BlockSpec(memory_space=pltpu.VMEM)
    return pl.pallas_call(
        functools.partial(attention_kernel, halo_span),
        out_shape=(
            jax.ShapeDtypeStruct((rows, q_cols), jnp.bfloat16),
            jax.ShapeDtypeStruct((rows, q_cols), jnp.bfloat16),
            jax.ShapeDtypeStruct((rows, 2 * d), jnp.float32),
        )
        + (jax.ShapeDtypeStruct((rows, 2 * d), jnp.bfloat16),) * halo_span,
        in_specs=[pl.BlockSpec(memory_space=pltpu.SMEM)] + [vmem] * (halo_span + 3),
        out_specs=(vmem,) * (3 + halo_span),
        scratch_shapes=[
            pltpu.VMEM((ext, 2 * d), jnp.bfloat16),
            pltpu.VMEM((2 * d, ext), jnp.bfloat16),
            pltpu.VMEM((ext, 2 * d), jnp.float32),
            pltpu.VMEM((window, Q_PER_KV * TILE), jnp.float32),
        ],
        cost_estimate=pl.CostEstimate(
            flops=10 * elems * d, bytes_accessed=6 * rows * 1024, transcendentals=elems
        ),
        compiler_params=pltpu.CompilerParams(vmem_limit_bytes=32 * 1024 * 1024),
    )(key_start, qkv, *kv_list, grad_out)


def per_device(normed, cotangent, qkv_master, adam_first, adam_second, skip_flag, scale_exponent):
    tok_rows = normed.shape[0]
    kv_groups = qkv_master.shape[1]
    d = HEAD_DIM
    q_cols = Q_PER_KV * d
    halo_span = ATTEND_SPAN // tok_rows
    head_count = lax.axis_size("head")
    head_pos = lax.axis_index("head")
    part_rows = tok_rows // head_count
    key_start = (lax.axis_index("seq") * tok_rows - halo_span * tok_rows).astype(jnp.int32)
    key_start = key_start.reshape(1)
    scale_power = jnp.left_shift(jnp.int32(1), scale_exponent[0]).astype(jnp.float32)
    grad_out = (cotangent.astype(jnp.float32) * scale_power).astype(jnp.bfloat16)

    weights = [
        lax.all_gather(qkv_master[:, g, :].astype(jnp.bfloat16), "seq", axis=0, tiled=True)
        for g in range(kv_groups)
    ]
    outs, sums = [], []
    own_part = peer_part = None
    for g in range(kv_groups):
        qkv = dot_nn(normed, weights[g])
        k_raw = qkv[:, q_cols : q_cols + d]
        k_unit, k_factor = head_norm(k_raw)
        kv = jnp.concatenate([k_unit, qkv[:, q_cols + d :]], 1).astype(jnp.bfloat16)
        kv_list = [shifted(kv, "seq", s) for s in range(halo_span, 0, -1)] + [kv]
        out, gq, own, *backs = group_attention(
            qkv, kv_list, grad_out[:, g * q_cols : (g + 1) * q_cols], key_start
        )
        outs.append(out)
        for s in range(1, halo_span + 1):
            own = own + shifted(backs[s - 1], "seq", -s).astype(jnp.float32)
        gk = norm_back(k_raw, k_factor, own[:, :d])
        grad_qkv = jnp.concatenate([gq, gk.astype(jnp.bfloat16), own[:, d:].astype(jnp.bfloat16)], 1)
        term = lax.dot_general(
            normed, grad_qkv, (((0,), (0,)), ((), ())), preferred_element_type=jnp.float32
        )
        sums.append(
            lax.psum_scatter(
                term.astype(jnp.bfloat16), "seq", scatter_dimension=0, tiled=True
            ).astype(jnp.float32)
        )
        if head_count == 2:
            peer_rows = lax.dynamic_slice_in_dim(grad_qkv, (1 - head_pos) * part_rows, part_rows, 0)
            own_rows = lax.dynamic_slice_in_dim(grad_qkv, head_pos * part_rows, part_rows, 0)
            peer_term = dot_nt(peer_rows, weights[g])
            peer_part = peer_term if peer_part is None else peer_part + peer_term
        else:
            own_rows = grad_qkv
        own_term = dot_nt(own_rows, weights[g])
        own_part = own_term if own_part is None else own_part + own_term
    if head_count == 2:
        far_part = lax.ppermute(peer_part.astype(jnp.bfloat16), "head", [(0, 1), (1, 0)])
        d_tokens = own_part + far_part.astype(jnp.float32)
    else:
        d_tokens = lax.psum_scatter(own_part, "head", scatter_dimension=0, tiled=True)
    d_tokens = d_tokens.astype(jnp.bfloat16)
    attn_out = jnp.concatenate(outs, 1)
    gradient = jnp.stack(sums, 1) / scale_power
    first_new = beta_one * adam_first + (1.0 - beta_one) * gradient
    second_new = beta_two * adam_second + (1.0 - beta_two) * gradient * gradient
    first_fix = 1.0 - beta_one**ADAM_STEP
    second_fix = 1.0 - beta_two**ADAM_STEP
    update = first_new / first_fix / (jnp.sqrt(second_new / second_fix) + adam_eps)
    master_new = qkv_master - learn_rate * (update + weight_decay * qkv_master)
    own_flags = lax.dynamic_slice_in_dim(skip_flag, head_pos * kv_groups, kv_groups, 0)
    applied = (own_flags == 0)[None, :, None]
    return (
        attn_out,
        d_tokens,
        jnp.where(applied, master_new, qkv_master),
        jnp.where(applied, first_new, adam_first),
        jnp.where(applied, second_new, adam_second),
    )


def solution(mesh):
    return jax.shard_map(
        per_device,
        mesh=mesh,
        in_specs=(
            P("seq", None),
            P("seq", "head"),
            P("seq", "head", None),
            P("seq", "head", None),
            P("seq", "head", None),
            P(),
            P(),
        ),
        out_specs=(
            P("seq", "head"),
            P(("seq", "head"), None),
            P("seq", "head", None),
            P("seq", "head", None),
            P("seq", "head", None),
        ),
        check_vma=False,
    )
```

time: 1380 us -> 658 us (0.48)
  waiting for transfers between devices: 1060 us -> 377 us
  other arithmetic: 60.5 us -> 12.9 us
  Pallas kernels: 0 us -> 42.7 us
  matrix products: 108 us -> 80.8 us
  local copies, waits for them, and re-layouts: 97.3 us -> 72.7 us
    all_to_all x1 -> x0, waiting for transfers between devices: 792 us -> none  [per_device(): lax.all_to_all(whole_term, 'seq', split_axis=0, concat_axis=0, tiled=True)]
    unnamed x2 -> x12, waiting for transfers between devices: 0.03 us -> 183 us
    reduce_scatter x1 -> x0, waiting for transfers between devices: 125 us -> none  [per_device(): lax.psum_scatter(lax.dot_general(row_part, full16, (((1,), (1,)), ((), ()...]
    ppermute x8 -> x16, waiting for transfers between devices: 26.4 us -> 109 us  [shifted(): return lax.ppermute(block, axis, route)]
    unnamed x36 -> x53, local copies, waits for them, and re-layouts: 8.77 us -> 70.2 us
    all_gather x1 -> x4, waiting for transfers between devices: 113 us -> 56 us  [per_device(): lax.all_gather(qkv_master[:, g, :].astype(jnp.bfloat16), 'seq', axis=0, t...]
    dot_general x1 -> x0, local copies, waits for them, and re-layouts: 42.8 us -> none  [per_device(): lax.dot_general(row_part, grad_qkv, (((0,), (0,)), ((), ())), preferred_e...]
    pallas_call x0 -> x4, Pallas kernels: none -> 42.7 us  [group_attention(): pl.pallas_call(functools.partial(attention_kernel, halo_span), out_shape=...]
  transfers between devices with their start and end apart: 11 -> 25, of which waited for: 6 -> 21; matrix products, arithmetic and copies ran while one was open for 8% -> 21% of each run, Pallas kernels for 0% -> 7%
where the time goes in v1:
time: 658 us; the launch traced here: 647 us
  waiting for transfers between devices  377 us (57%)
  matrix products  80.8 us (12%)
  local copies, waits for them, and re-layouts  72.7 us (11%)
  starting transfers between devices  44.7 us (7%)
  Pallas kernels  42.7 us (6%)
  between operations  16 us (2%)
  other arithmetic  12.9 us (2%)
    unnamed x12, waiting for transfers between devices  183 us
    ppermute x16, waiting for transfers between devices, shifted(): return lax.ppermute(block, axis, route)  109 us
    unnamed x53, local copies, waits for them, and re-layouts  70.2 us
    all_gather x4, waiting for transfers between devices, per_device(): lax.all_gather(qkv_master[:, g, :].astype(jnp.bfloat16), 'seq', axis=0, t...  56 us
    pallas_call x4, Pallas kernels, group_attention(): pl.pallas_call(functools.partial(attention_kernel, halo_span), out_shape=...  42.7 us
    ppermute x16, starting transfers between devices, shifted(): return lax.ppermute(block, axis, route)  42.5 us
    dot_general x8, matrix products, dot_nt(): lax.dot_general(a, b, (((1,), (1,)), ((), ())), preferred_element_type=jn...  30.7 us
    ppermute x1, waiting for transfers between devices, per_device(): lax.ppermute(peer_part.astype(jnp.bfloat16), 'head', [(0, 1), (1, 0)])  29.9 us
  transfers between devices with their start and end apart: 25, of which 21 were waited for; matrix products, arithmetic and copies ran while one was open for 21% of the time, Pallas kernels for 7%

profile of v1, /device:TPU:8, one launch (start us, length us, event | category | flops | bytes accessed | tf_op | source)
XLA Modules:
  0.0 647.0 jit_solution(853325262801576385)
XLA Ops:
  13.6 56.0 %all-gather.15.cloned.1.call-done = bf16[5376,1,512]{2,0,1:T(8,128)(2,1)} async-done(((bf16[336,1,512]{2,0,1:T(8,128)(2,1)}), bf16[5376,1,512]{2,0,1:T(8,128)(2,1)}) %all-gather.15.cloned.1.call-update) | async-done | bytes 5505040 | tf_op jit(solution)/shard_map/all_gather | solution.py:172
  83.6 10.3 %collective-permute-done.6.refs_0_ = bf16[512,256]{1,0:T(8,128)(2,1)S(1)} collective-permute-done((bf16[512,256]{1,0:T(8,128)(2,1)S(1)}, bf16[512,256]{1,0:T(8,128)(2,1)S(1)}, u32[]{:S(2)}, u32[]{:S(2)}) %collective-permute-start.6) | collective-permute-done | bytes 262176 | tf_op jit(solution)/shard_map/ppermute | solution.py:31
  94.0 7.4 %collective-permute-done.7.refs_1_ = bf16[512,256]{1,0:T(8,128)(2,1)S(1)} collective-permute-done((bf16[512,256]{1,0:T(8,128)(2,1)S(1)}, bf16[512,256]{1,0:T(8,128)(2,1)S(1)}, u32[]{:S(2)}, u32[]{:S(2)}) %collective-permute-start.7) | collective-permute-done | bytes 262176 | tf_op jit(solution)/shard_map/ppermute | solution.py:31
  101.4 10.7 %shard_map.113 = (bf16[512,256]{1,0:T(8,128)(2,1)S(1)}, bf16[512,256]{1,0:T(8,128)(2,1)S(1)}, f32[512,256]{1,0:T(8,128)S(1)}, bf16[512,256]{1,0:T(8,128)(2,1)S(1)}, bf16[512,256]{1,0:T(8,128)(2,1)S(1)}) custom-call(s32[1]{0:T(128)} %bitcast.start_ref, f32[512,512]{1,0:T(8,128)S(1)} %fusion.7.qkv_ref, bf16[512,256]{1,0:T(8,128)(2,1)S(1)} %collective-permute-done.6.refs_0_, ...), custom_call_target="tpu_custom_call" | custom-call | flops 1509949440 | bytes 3145728 | tf_op jit(solution)/shard_map/pallas_call | solution.py:134
  116.2 11.6 %collective-permute-done.15 = bf16[512,256]{1,0:T(8,128)(2,1)S(1)} collective-permute-done((bf16[512,256]{1,0:T(8,128)(2,1)S(1)}, bf16[512,256]{1,0:T(8,128)(2,1)S(1)}, u32[]{:S(2)}, u32[]{:S(2)}) %collective-permute-start.15) | collective-permute-done | bytes 262176 | tf_op jit(solution)/shard_map/ppermute | solution.py:31
  129.5 7.5 %fusion.3 = bf16[5376,512]{0,1:T(8,128)(2,1)} fusion(bf16[512,5376]{1,0:T(8,128)(2,1)} %param.7, bf16[512,128]{1,0:T(8,128)(2,1)S(1)} %slice.164, bf16[512,128]{1,0:T(8,128)(2,1)S(1)} %subtract_convert_fusion, bf16[512,256]{1,0:T(8,128)(2,1)S(1)} %get-tuple-element.41), kind=kOutput, calls=%fused_computation.13 | convolution fusion | flops 2822897664 | bytes 11534336 | tf_op jit(solution)/shard_map/dot_general | solution.py:191
  136.9 8.2 %copy.90 = bf16[5376,512]{1,0:T(8,128)(2,1)} copy(bf16[5376,512]{0,1:T(8,128)(2,1)} %fusion.3) | data formatting | bytes 11010048
  159.6 10.0 %collective-permute-done.4.refs_0_ = bf16[512,256]{1,0:T(8,128)(2,1)S(1)} collective-permute-done((bf16[512,256]{1,0:T(8,128)(2,1)S(1)}, bf16[512,256]{1,0:T(8,128)(2,1)S(1)}, u32[]{:S(2)}, u32[]{:S(2)}) %collective-permute-start.4) | collective-permute-done | bytes 262176 | tf_op jit(solution)/shard_map/ppermute | solution.py:31
  173.7 10.7 %shard_map.112 = (bf16[512,256]{1,0:T(8,128)(2,1)S(1)}, bf16[512,256]{1,0:T(8,128)(2,1)S(1)}, f32[512,256]{1,0:T(8,128)S(1)}, bf16[512,256]{1,0:T(8,128)(2,1)S(1)}, bf16[512,256]{1,0:T(8,128)(2,1)S(1)}) custom-call(s32[1]{0:T(128)} %bitcast.start_ref, f32[512,512]{1,0:T(8,128)S(1)} %fusion.11.qkv_ref, bf16[512,256]{1,0:T(8,128)(2,1)S(1)} %collective-permute-done.4.refs_0_, ...), custom_call_target="tpu_custom_call" | custom-call | flops 1509949440 | bytes 3145728 | tf_op jit(solution)/shard_map/pallas_call | solution.py:134
  188.7 9.5 %collective-permute-done.13 = bf16[512,256]{1,0:T(8,128)(2,1)S(1)} collective-permute-done((bf16[512,256]{1,0:T(8,128)(2,1)S(1)}, bf16[512,256]{1,0:T(8,128)(2,1)S(1)}, u32[]{:S(2)}, u32[]{:S(2)}) %collective-permute-start.13) | collective-permute-done | bytes 262176 | tf_op jit(solution)/shard_map/ppermute | solution.py:31
  207.9 8.2 %copy.88 = bf16[5376,512]{1,0:T(8,128)(2,1)} copy(bf16[5376,512]{0,1:T(8,128)(2,1)} %fusion.2) | data formatting | bytes 11010048
  231.2 8.4 %collective-permute-done.2.refs_0_ = bf16[512,256]{1,0:T(8,128)(2,1)S(1)} collective-permute-done((bf16[512,256]{1,0:T(8,128)(2,1)S(1)}, bf16[512,256]{1,0:T(8,128)(2,1)S(1)}, u32[]{:S(2)}, u32[]{:S(2)}) %collective-permute-start.2) | collective-permute-done | bytes 262176 | tf_op jit(solution)/shard_map/ppermute | solution.py:31
  242.6 10.7 %shard_map.111 = (bf16[512,256]{1,0:T(8,128)(2,1)S(1)}, bf16[512,256]{1,0:T(8,128)(2,1)S(1)}, f32[512,256]{1,0:T(8,128)S(1)}, bf16[512,256]{1,0:T(8,128)(2,1)S(1)}, bf16[512,256]{1,0:T(8,128)(2,1)S(1)}) custom-call(s32[1]{0:T(128)} %bitcast.start_ref, f32[512,512]{1,0:T(8,128)S(1)} %fusion.15.qkv_ref, bf16[512,256]{1,0:T(8,128)(2,1)S(1)} %collective-permute-done.2.refs_0_, ...), custom_call_target="tpu_custom_call" | custom-call | flops 1509949440 | bytes 3145728 | tf_op jit(solution)/shard_map/pallas_call | solution.py:134
  257.3 8.4 %collective-permute-done.11 = bf16[512,256]{1,0:T(8,128)(2,1)S(1)} collective-permute-done((bf16[512,256]{1,0:T(8,128)(2,1)S(1)}, bf16[512,256]{1,0:T(8,128)(2,1)S(1)}, u32[]{:S(2)}, u32[]{:S(2)}) %collective-permute-start.11) | collective-permute-done | bytes 262176 | tf_op jit(solution)/shard_map/ppermute | solution.py:31
  265.7 8.1 %collective-permute-done.10 = bf16[512,256]{1,0:T(8,128)(2,1)S(1)} collective-permute-done((bf16[512,256]{1,0:T(8,128)(2,1)S(1)}, bf16[512,256]{1,0:T(8,128)(2,1)S(1)}, u32[]{:S(2)}, u32[]{:S(2)}) %collective-permute-start.10) | collective-permute-done | bytes 262176 | tf_op jit(solution)/shard_map/ppermute | solution.py:31
  279.3 8.3 %copy.86 = bf16[5376,512]{1,0:T(8,128)(2,1)} copy(bf16[5376,512]{0,1:T(8,128)(2,1)} %fusion.1) | data formatting | bytes 11010048
  310.0 10.7 %shard_map.110 = (bf16[512,256]{1,0:T(8,128)(2,1)S(1)}, bf16[512,256]{1,0:T(8,128)(2,1)S(1)}, f32[512,256]{1,0:T(8,128)S(1)}, bf16[512,256]{1,0:T(8,128)(2,1)S(1)}, bf16[512,256]{1,0:T(8,128)(2,1)S(1)}) custom-call(s32[1]{0:T(128)} %bitcast.start_ref, f32[512,512]{1,0:T(8,128)S(1)} %fusion.21.qkv_ref, bf16[512,256]{1,0:T(8,128)(2,1)S(1)} %collective-permute-done.refs_0_, ...), custom_call_target="tpu_custom_call" | custom-call | flops 1509949440 | bytes 3145728 | tf_op jit(solution)/shard_map/pallas_call | solution.py:134
  324.7 8.1 %collective-permute-done.9 = bf16[512,256]{1,0:T(8,128)(2,1)S(1)} collective-permute-done((bf16[512,256]{1,0:T(8,128)(2,1)S(1)}, bf16[512,256]{1,0:T(8,128)(2,1)S(1)}, u32[]{:S(2)}, u32[]{:S(2)}) %collective-permute-start.9) | collective-permute-done | bytes 262176 | tf_op jit(solution)/shard_map/ppermute | solution.py:31
  344.7 8.3 %copy.84 = bf16[5376,512]{1,0:T(8,128)(2,1)} copy(bf16[5376,512]{0,1:T(8,128)(2,1)} %fusion) | data formatting | bytes 11010048
  397.2 29.9 %collective-permute-done.16 = bf16[256,5376]{1,0:T(8,128)(2,1)} collective-permute-done((bf16[256,5376]{1,0:T(8,128)(2,1)}, bf16[256,5376]{1,0:T(8,128)(2,1)}, u32[]{:S(2)}, u32[]{:S(2)}) %collective-permute-start.16) | collective-permute-done | bytes 2752544 | tf_op jit(solution)/shard_map/ppermute | solution.py:209
  433.6 16.4 %reduce-scatter.17.cloned.1.call-done = bf16[336,512]{1,0:T(8,128)(2,1)} async-done(((bf16[5376,512]{1,0:T(8,128)(2,1)}), bf16[336,512]{1,0:T(8,128)(2,1)}) %reduce-scatter.17.cloned.1.call-update) | async-done | bytes 344080
  451.2 81.6 %reduce-scatter.15.cloned.1.call-done = bf16[336,512]{1,0:T(8,128)(2,1)} async-done(((bf16[5376,512]{1,0:T(8,128)(2,1)}), bf16[336,512]{1,0:T(8,128)(2,1)}) %reduce-scatter.15.cloned.1.call-update) | async-done | bytes 344080
  534.0 82.6 %reduce-scatter.13.cloned.1.call-done = bf16[336,512]{1,0:T(8,128)(2,1)} async-done(((bf16[5376,512]{1,0:T(8,128)(2,1)}), bf16[336,512]{1,0:T(8,128)(2,1)}) %reduce-scatter.13.cloned.1.call-update) | async-done | bytes 344080
  617.8 7.3 %fusion.25 = (f32[336,4,512]{0,2,1:T(8,128)}, f32[336,4,512]{0,2,1:T(8,128)}, f32[336,4,512]{0,2,1:T(8,128)}) fusion(f32[336,4,512]{0,2,1:T(8,128)} %copy.71, pred[4]{0:T(512)(128)(4,1)S(1)} %dynamic-slice_compare_fusion, f32[]{:T(128)} %bitcast.2, bf16[336,1,512]{0,2,1:T(8,128)(2,1)S(1)} %bitcast.70, bf16[336,1,512]{0,2,1:T(8,128)(2,1)S(1)} %bitcast.71, ...), kind=kLoop, calls=%fused_computation.41 | loop fusion | flops 14450688 | bytes 17891336 | tf_op jit(solution)/shard_map/jit(_where)/select_n | solution.py:229
  (164 shorter events, 192.1 us)
Async XLA Ops:
  7.2 62.4 %all-gather.15.cloned.1.call-start = ((), (), s32[]{:S(2)}) async-start(), calls=%async_computation.7 | async-start | bytes 5849088 | tf_op jit(solution)/shard_map/all_gather | solution.py:172
  10.9 134.3 %all-gather.13.cloned.1.call-start = ((), (), s32[]{:S(2)}) async-start(), calls=%async_computation.6 | async-start | bytes 5849088 | tf_op jit(solution)/shard_map/all_gather | solution.py:172
  11.6 204.7 %all-gather.11.cloned.1.call-start = ((), (), s32[]{:S(2)}) async-start(), calls=%async_computation.5 | async-start | bytes 5849088 | tf_op jit(solution)/shard_map/all_gather | solution.py:172
  12.4 275.4 %all-gather.9.cloned.1.call-start = ((), (), s32[]{:S(2)}) async-start(), calls=%async_computation.4 | async-start | bytes 5849088 | tf_op jit(solution)/shard_map/all_gather | solution.py:172
  12.9 419.5 %reduce-scatter.19.cloned.1.call-start = ((), (), s32[]{:S(2)}) async-start(), calls=%async_computation.11 | async-start | bytes 5849088
  76.8 17.2 %collective-permute-start.6 = (bf16[512,256]{1,0:T(8,128)(2,1)S(1)}, bf16[512,256]{1,0:T(8,128)(2,1)S(1)}, u32[]{:S(2)}, u32[]{:S(2)}) collective-permute-start(bf16[512,256]{1,0:T(8,128)(2,1)S(1)} %pad_maximum_fusion.8.refs_2_), channel_id=1, source_target_pairs={{0,4},{2,6},{4,8},{6,10},{8,12},{10,14},{12,16},{14,18},{16,20},{1... | collective-permute-start | bytes 786440 | tf_op jit(solution)/shard_map/ppermute | solution.py:31
  79.2 22.2 %collective-permute-start.7 = (bf16[512,256]{1,0:T(8,128)(2,1)S(1)}, bf16[512,256]{1,0:T(8,128)(2,1)S(1)}, u32[]{:S(2)}, u32[]{:S(2)}) collective-permute-start(bf16[512,256]{1,0:T(8,128)(2,1)S(1)} %pad_maximum_fusion.8.refs_2_), channel_id=1, source_target_pairs={{0,2},{2,4},{4,6},{6,8},{8,10},{10,12},{12,14},{14,16},{16,18},{18... | collective-permute-start | bytes 786440 | tf_op jit(solution)/shard_map/ppermute | solution.py:31
  112.1 15.6 %collective-permute-start.15 = (bf16[512,256]{1,0:T(8,128)(2,1)S(1)}, bf16[512,256]{1,0:T(8,128)(2,1)S(1)}, u32[]{:S(2)}, u32[]{:S(2)}) collective-permute-start(bf16[512,256]{1,0:T(8,128)(2,1)S(1)} %get-tuple-element.44), channel_id=1, source_target_pairs={{4,0},{6,2},{8,4},{10,6},{12,8},{14,10},{16,12},{18,14},{20,16},{2... | collective-permute-start | bytes 786440 | tf_op jit(solution)/shard_map/ppermute | solution.py:31
  114.0 15.0 %collective-permute-start.14 = (bf16[512,256]{1,0:T(8,128)(2,1)S(1)}, bf16[512,256]{1,0:T(8,128)(2,1)S(1)}, u32[]{:S(2)}, u32[]{:S(2)}) collective-permute-start(bf16[512,256]{1,0:T(8,128)(2,1)S(1)} %get-tuple-element.43), channel_id=1, source_target_pairs={{2,0},{4,2},{6,4},{8,6},{10,8},{12,10},{14,12},{16,14},{18,16},{20... | collective-permute-start | bytes 786440 | tf_op jit(solution)/shard_map/ppermute | solution.py:31
  145.1 304.9 %reduce-scatter.17.cloned.1.call-start = ((), (), s32[]{:S(2)}) async-start(), calls=%async_computation.10 | async-start | bytes 5849088
  152.3 17.3 %collective-permute-start.4 = (bf16[512,256]{1,0:T(8,128)(2,1)S(1)}, bf16[512,256]{1,0:T(8,128)(2,1)S(1)}, u32[]{:S(2)}, u32[]{:S(2)}) collective-permute-start(bf16[512,256]{1,0:T(8,128)(2,1)S(1)} %pad_maximum_fusion.7.refs_2_), channel_id=1, source_target_pairs={{0,4},{2,6},{4,8},{6,10},{8,12},{10,14},{12,16},{14,18},{16,20},{1... | collective-permute-start | bytes 786440 | tf_op jit(solution)/shard_map/ppermute | solution.py:31
  156.1 17.6 %collective-permute-start.5 = (bf16[512,256]{1,0:T(8,128)(2,1)S(1)}, bf16[512,256]{1,0:T(8,128)(2,1)S(1)}, u32[]{:S(2)}, u32[]{:S(2)}) collective-permute-start(bf16[512,256]{1,0:T(8,128)(2,1)S(1)} %pad_maximum_fusion.7.refs_2_), channel_id=1, source_target_pairs={{0,2},{2,4},{4,6},{6,8},{8,10},{10,12},{12,14},{14,16},{16,18},{18... | collective-permute-start | bytes 786440 | tf_op jit(solution)/shard_map/ppermute | solution.py:31
  184.4 13.8 %collective-permute-start.13 = (bf16[512,256]{1,0:T(8,128)(2,1)S(1)}, bf16[512,256]{1,0:T(8,128)(2,1)S(1)}, u32[]{:S(2)}, u32[]{:S(2)}) collective-permute-start(bf16[512,256]{1,0:T(8,128)(2,1)S(1)} %get-tuple-element.40), channel_id=1, source_target_pairs={{4,0},{6,2},{8,4},{10,6},{12,8},{14,10},{16,12},{18,14},{20,16},{2... | collective-permute-start | bytes 786440 | tf_op jit(solution)/shard_map/ppermute | solution.py:31
  186.3 16.0 %collective-permute-start.12 = (bf16[512,256]{1,0:T(8,128)(2,1)S(1)}, bf16[512,256]{1,0:T(8,128)(2,1)S(1)}, u32[]{:S(2)}, u32[]{:S(2)}) collective-permute-start(bf16[512,256]{1,0:T(8,128)(2,1)S(1)} %get-tuple-element.39), channel_id=1, source_target_pairs={{2,0},{4,2},{6,4},{8,6},{10,8},{12,10},{14,12},{16,14},{18,16},{20... | collective-permute-start | bytes 786440 | tf_op jit(solution)/shard_map/ppermute | solution.py:31
  216.2 316.6 %reduce-scatter.15.cloned.1.call-start = ((), (), s32[]{:S(2)}) async-start(), calls=%async_computation.9 | async-start | bytes 5849088
  223.4 16.2 %collective-permute-start.2 = (bf16[512,256]{1,0:T(8,128)(2,1)S(1)}, bf16[512,256]{1,0:T(8,128)(2,1)S(1)}, u32[]{:S(2)}, u32[]{:S(2)}) collective-permute-start(bf16[512,256]{1,0:T(8,128)(2,1)S(1)} %pad_maximum_fusion.6.refs_2_), channel_id=1, source_target_pairs={{0,4},{2,6},{4,8},{6,10},{8,12},{10,14},{12,16},{14,18},{16,20},{1... | collective-permute-start | bytes 786440 | tf_op jit(solution)/shard_map/ppermute | solution.py:31
  225.6 17.0 %collective-permute-start.3 = (bf16[512,256]{1,0:T(8,128)(2,1)S(1)}, bf16[512,256]{1,0:T(8,128)(2,1)S(1)}, u32[]{:S(2)}, u32[]{:S(2)}) collective-permute-start(bf16[512,256]{1,0:T(8,128)(2,1)S(1)} %pad_maximum_fusion.6.refs_2_), channel_id=1, source_target_pairs={{0,2},{2,4},{4,6},{6,8},{8,10},{10,12},{12,14},{14,16},{16,18},{18... | collective-permute-start | bytes 786440 | tf_op jit(solution)/shard_map/ppermute | solution.py:31
  253.3 12.4 %collective-permute-start.11 = (bf16[512,256]{1,0:T(8,128)(2,1)S(1)}, bf16[512,256]{1,0:T(8,128)(2,1)S(1)}, u32[]{:S(2)}, u32[]{:S(2)}) collective-permute-start(bf16[512,256]{1,0:T(8,128)(2,1)S(1)} %get-tuple-element.36), channel_id=1, source_target_pairs={{4,0},{6,2},{8,4},{10,6},{12,8},{14,10},{16,12},{18,14},{20,16},{2... | collective-permute-start | bytes 786440 | tf_op jit(solution)/shard_map/ppermute | solution.py:31
  255.2 18.5 %collective-permute-start.10 = (bf16[512,256]{1,0:T(8,128)(2,1)S(1)}, bf16[512,256]{1,0:T(8,128)(2,1)S(1)}, u32[]{:S(2)}, u32[]{:S(2)}) collective-permute-start(bf16[512,256]{1,0:T(8,128)(2,1)S(1)} %get-tuple-element.35), channel_id=1, source_target_pairs={{2,0},{4,2},{6,4},{8,6},{10,8},{12,10},{14,12},{16,14},{18,16},{20... | collective-permute-start | bytes 786440 | tf_op jit(solution)/shard_map/ppermute | solution.py:31
  287.7 328.9 %reduce-scatter.13.cloned.1.call-start = ((), (), s32[]{:S(2)}) async-start(), calls=%async_computation.8 | async-start | bytes 5849088
  297.6 12.4 %collective-permute-start.1 = (bf16[512,256]{1,0:T(8,128)(2,1)S(1)}, bf16[512,256]{1,0:T(8,128)(2,1)S(1)}, u32[]{:S(2)}, u32[]{:S(2)}) collective-permute-start(bf16[512,256]{1,0:T(8,128)(2,1)S(1)} %pad_maximum_fusion.5.refs_2_), channel_id=1, source_target_pairs={{0,2},{2,4},{4,6},{6,8},{8,10},{10,12},{12,14},{14,16},{16,18},{18... | collective-permute-start | bytes 786440 | tf_op jit(solution)/shard_map/ppermute | solution.py:31
  320.7 12.2 %collective-permute-start.9 = (bf16[512,256]{1,0:T(8,128)(2,1)S(1)}, bf16[512,256]{1,0:T(8,128)(2,1)S(1)}, u32[]{:S(2)}, u32[]{:S(2)}) collective-permute-start(bf16[512,256]{1,0:T(8,128)(2,1)S(1)} %get-tuple-element.32), channel_id=1, source_target_pairs={{4,0},{6,2},{8,4},{10,6},{12,8},{14,10},{16,12},{18,14},{20,16},{2... | collective-permute-start | bytes 786440 | tf_op jit(solution)/shard_map/ppermute | solution.py:31
  322.6 16.6 %collective-permute-start.8 = (bf16[512,256]{1,0:T(8,128)(2,1)S(1)}, bf16[512,256]{1,0:T(8,128)(2,1)S(1)}, u32[]{:S(2)}, u32[]{:S(2)}) collective-permute-start(bf16[512,256]{1,0:T(8,128)(2,1)S(1)} %get-tuple-element.31), channel_id=1, source_target_pairs={{2,0},{4,2},{6,4},{8,6},{10,8},{12,10},{14,12},{16,14},{18,16},{20... | collective-permute-start | bytes 786440 | tf_op jit(solution)/shard_map/ppermute | solution.py:31
  368.4 58.7 %collective-permute-start.16 = (bf16[256,5376]{1,0:T(8,128)(2,1)}, bf16[256,5376]{1,0:T(8,128)(2,1)}, u32[]{:S(2)}, u32[]{:S(2)}) collective-permute-start(bf16[256,5376]{1,0:T(8,128)(2,1)} %fusion.4), channel_id=1, source_target_pairs={{0,1},{1,0},{2,3},{3,2},{4,5},{5,4},{6,7},{7,6},{8,9},{9,8},{10,11... | collective-permute-start | bytes 8257544 | tf_op jit(solution)/shard_map/ppermute | solution.py:209
  (20 other events, 386.8 us)
Sparse Core Ops, SparseCore 0:
  11.0 58.5 all-gather.14
  72.5 69.2 all-gather.12
  144.7 66.0 all-gather.10
  213.5 64.6 all-gather.8
  281.9 84.3 reduce-scatter.18
  370.6 79.3 reduce-scatter.16
  453.9 78.8 reduce-scatter.14
  537.2 79.3 reduce-scatter.12

commit v2 on v1

--- a/solution.py
+++ b/solution.py
@@ -127,20 +127,30 @@
     halo_span = len(kv_list) - 1
     d = HEAD_DIM
     q_cols = Q_PER_KV * d
+    groups = grad_out.shape[1] // q_cols
     ext = (halo_span + 1) * rows
     window = ATTEND_SPAN + TILE
-    elems = Q_PER_KV * rows * window
-    vmem = pl.BlockSpec(memory_space=pltpu.VMEM)
+    elems = groups * Q_PER_KV * rows * window
+
+    def block(cols):
+        return pl.BlockSpec((rows, cols), lambda g: (0, g))
+
+    def result(cols, kind):
+        return jax.ShapeDtypeStruct((rows, groups * cols), kind)
+
     return pl.pallas_call(
         functools.partial(attention_kernel, halo_span),
+        grid=(groups,),
         out_shape=(
-            jax.ShapeDtypeStruct((rows, q_cols), jnp.bfloat16),
-            jax.ShapeDtypeStruct((rows, q_cols), jnp.bfloat16),
-            jax.ShapeDtypeStruct((rows, 2 * d), jnp.float32),
-        )
-        + (jax.ShapeDtypeStruct((rows, 2 * d), jnp.bfloat16),) * halo_span,
-        in_specs=[pl.BlockSpec(memory_space=pltpu.SMEM)] + [vmem] * (halo_span + 3),
-        out_specs=(vmem,) * (3 + halo_span),
+            result(q_cols, jnp.bfloat16),
+            result(q_cols, jnp.bfloat16),
+            result(2 * d, jnp.float32),
+        )
+        + (result(2 * d, jnp.bfloat16),) * halo_span,
+        in_specs=[pl.BlockSpec(memory_space=pltpu.SMEM), block(q_cols + 2 * d)]
+        + [block(2 * d)] * (halo_span + 1)
+        + [block(q_cols)],
+        out_specs=(block(q_cols), block(q_cols), block(2 * d)) + (block(2 * d),) * halo_span,
         scratch_shapes=[
             pltpu.VMEM((ext, 2 * d), jnp.bfloat16),
             pltpu.VMEM((2 * d, ext), jnp.bfloat16),
@@ -148,15 +158,107 @@
             pltpu.VMEM((window, Q_PER_KV * TILE), jnp.float32),
         ],
         cost_estimate=pl.CostEstimate(
-            flops=10 * elems * d, bytes_accessed=6 * rows * 1024, transcendentals=elems
+            flops=10 * elems * d,
+            bytes_accessed=groups * 6 * rows * 1024,
+            transcendentals=elems,
         ),
         compiler_params=pltpu.CompilerParams(vmem_limit_bytes=32 * 1024 * 1024),
     )(key_start, qkv, *kv_list, grad_out)
 
 
+def row_blocks(normed, own_rows):
+    seq_size = lax.axis_size("seq")
+    seq_pos = lax.axis_index("seq")
+    core, mid = seq_pos % 2, (seq_pos // 2) % 2
+    outer = seq_size // 4
+    rows = normed.T.reshape(outer, 2, 2, own_rows, normed.shape[0])
+
+    def pick(mid_at, core_at):
+        part = lax.dynamic_index_in_dim(rows, core_at, 2, keepdims=False)
+        part = lax.dynamic_index_in_dim(part, mid_at, 1, keepdims=False)
+        return part.reshape(outer * own_rows, normed.shape[0])
+
+    other_core = jnp.concatenate([pick(1 - mid, 1 - core), pick(mid, 1 - core)], 0)
+    return other_core, pick(1 - mid, core), pick(mid, core)
+
+
+def reduce_rows(blocks, grad_qkv):
+    other_core, other_chip, here = blocks
+    seq_size = lax.axis_size("seq")
+    outer_pos = lax.axis_index("seq") // 4
+    outer = seq_size // 4
+    devices = range(seq_size)
+    half = here.shape[0]
+    sent = dot_nn(other_core, grad_qkv).astype(jnp.bfloat16)
+    got = lax.ppermute(sent, "seq", [(i, i ^ 1) for i in devices])
+    sent = (dot_nn(other_chip, grad_qkv) + got[:half].astype(jnp.float32)).astype(jnp.bfloat16)
+    got_chip = lax.ppermute(sent, "seq", [(i, i ^ 2) for i in devices])
+    total = (
+        dot_nn(here, grad_qkv) + got[half:].astype(jnp.float32) + got_chip.astype(jnp.float32)
+    ).astype(jnp.bfloat16)
+    total = total.reshape(outer, half // outer, grad_qkv.shape[1])
+
+    def part(at):
+        return lax.dynamic_index_in_dim(total, at, 0, keepdims=False)
+
+    parts = [part(outer_pos)]
+    for step in range(1, outer):
+        route = [(i, (i + 4 * step) % seq_size) for i in devices]
+        got = lax.ppermute(part((outer_pos + step) % outer), "seq", route)
+        parts.append(got)
+    return total, parts
+
+
+def adam_kernel(part_count, flag_ref, scale_ref, *refs):
+    groups = flag_ref.shape[0]
+    part_refs = refs[: groups * part_count]
+    master_ref, first_ref, second_ref, *out_refs = refs[groups * part_count :]
+    first_fix = 1.0 - beta_one**ADAM_STEP
+    second_fix = 1.0 - beta_two**ADAM_STEP
+    for g in range(groups):
+        gradient = part_refs[g * part_count][...].astype(jnp.float32)
+        for ref in part_refs[g * part_count + 1 : (g + 1) * part_count]:
+            gradient = gradient + ref[...].astype(jnp.float32)
+        gradient = gradient * scale_ref[0]
+        master, first, second = master_ref[:, g, :], first_ref[:, g, :], second_ref[:, g, :]
+        first_new = beta_one * first + (1.0 - beta_one) * gradient
+        second_new = beta_two * second + (1.0 - beta_two) * gradient * gradient
+        update = first_new / first_fix / (jnp.sqrt(second_new / second_fix) + adam_eps)
+        master_new = master - learn_rate * (update + weight_decay * master)
+        applied = flag_ref[g] == 0
+        for ref, new, old in zip(
+            out_refs, (master_new, first_new, second_new), (master, first, second)
+        ):
+            ref[:, g, :] = jnp.where(applied, new, old)
+
+
+def adam_step(own_flags, inverse_scale, sums, *state):
+    own_rows, groups, cols = state[0].shape
+    part_count = len(sums[0])
+    rows = own_rows
+    for size in (112, 56, 48):
+        if own_rows % size == 0:
+            rows = size
+            break
+    smem = pl.BlockSpec(memory_space=pltpu.SMEM)
+    part = pl.BlockSpec((rows, cols), lambda i: (i, 0))
+    whole = pl.BlockSpec((rows, groups, cols), lambda i: (i, 0, 0))
+    return pl.pallas_call(
+        functools.partial(adam_kernel, part_count),
+        grid=(own_rows // rows,),
+        out_shape=(jax.ShapeDtypeStruct(state[0].shape, jnp.float32),) * 3,
+        in_specs=[smem, smem] + [part] * (groups * part_count) + [whole] * 3,
+        out_specs=(whole,) * 3,
+        cost_estimate=pl.CostEstimate(
+            flops=20 * state[0].size, bytes_accessed=32 * state[0].size, transcendentals=0
+        ),
+        compiler_params=pltpu.CompilerParams(vmem_limit_bytes=40 * 1024 * 1024),
+    )(own_flags, inverse_scale, *[p for parts in sums for p in parts], *state)
+
+
 def per_device(normed, cotangent, qkv_master, adam_first, adam_second, skip_flag, scale_exponent):
     tok_rows = normed.shape[0]
-    kv_groups = qkv_master.shape[1]
+    own_rows, kv_groups, group_cols = qkv_master.shape
     d = HEAD_DIM
     q_cols = Q_PER_KV * d
     halo_span = ATTEND_SPAN // tok_rows
@@ -168,66 +270,63 @@
     scale_power = jnp.left_shift(jnp.int32(1), scale_exponent[0]).astype(jnp.float32)
     grad_out = (cotangent.astype(jnp.float32) * scale_power).astype(jnp.bfloat16)
 
-    weights = [
-        lax.all_gather(qkv_master[:, g, :].astype(jnp.bfloat16), "seq", axis=0, tiled=True)
-        for g in range(kv_groups)
-    ]
-    outs, sums = [], []
-    own_part = peer_part = None
-    for g in range(kv_groups):
-        qkv = dot_nn(normed, weights[g])
-        k_raw = qkv[:, q_cols : q_cols + d]
-        k_unit, k_factor = head_norm(k_raw)
-        kv = jnp.concatenate([k_unit, qkv[:, q_cols + d :]], 1).astype(jnp.bfloat16)
+    master16 = qkv_master.astype(jnp.bfloat16).reshape(own_rows, kv_groups * group_cols)
+    weights = lax.all_gather(master16, "seq", axis=0, tiled=True)
+    blocks = row_blocks(normed, own_rows)
+    pair = 2 if kv_groups % 2 == 0 else 1
+    outs, grads, sums = [], [], []
+    for low in range(0, kv_groups, pair):
+        qkv = dot_nn(normed, weights[:, low * group_cols : (low + pair) * group_cols])
+        kv, k_saved = [], []
+        for g in range(pair):
+            at = g * group_cols + q_cols
+            k_raw = qkv[:, at : at + d]
+            k_unit, k_factor = head_norm(k_raw)
+            k_saved.append((k_raw, k_factor))
+            kv += [k_unit.astype(jnp.bfloat16), qkv[:, at + d : at + 2 * d].astype(jnp.bfloat16)]
+        kv = jnp.concatenate(kv, 1)
         kv_list = [shifted(kv, "seq", s) for s in range(halo_span, 0, -1)] + [kv]
         out, gq, own, *backs = group_attention(
-            qkv, kv_list, grad_out[:, g * q_cols : (g + 1) * q_cols], key_start
+            qkv, kv_list, grad_out[:, low * q_cols : (low + pair) * q_cols], key_start
         )
         outs.append(out)
         for s in range(1, halo_span + 1):
             own = own + shifted(backs[s - 1], "seq", -s).astype(jnp.float32)
-        gk = norm_back(k_raw, k_factor, own[:, :d])
-        grad_qkv = jnp.concatenate([gq, gk.astype(jnp.bfloat16), own[:, d:].astype(jnp.bfloat16)], 1)
-        term = lax.dot_general(
-            normed, grad_qkv, (((0,), (0,)), ((), ())), preferred_element_type=jnp.float32
-        )
-        sums.append(
-            lax.psum_scatter(
-                term.astype(jnp.bfloat16), "seq", scatter_dimension=0, tiled=True
-            ).astype(jnp.float32)
-        )
-        if head_count == 2:
-            peer_rows = lax.dynamic_slice_in_dim(grad_qkv, (1 - head_pos) * part_rows, part_rows, 0)
-            own_rows = lax.dynamic_slice_in_dim(grad_qkv, head_pos * part_rows, part_rows, 0)
-            peer_term = dot_nt(peer_rows, weights[g])
-            peer_part = peer_term if peer_part is None else peer_part + peer_term
-        else:
-            own_rows = grad_qkv
-        own_term = dot_nt(own_rows, weights[g])
-        own_part = own_term if own_part is None else own_part + own_term
+        for g in range(pair):
+            at = g * 2 * d
+            gk = norm_back(*k_saved[g], own[:, at : at + d])
+            grad_qkv = jnp.concatenate(
+                [
+                    gq[:, g * q_cols : (g + 1) * q_cols],
+                    gk.astype(jnp.bfloat16),
+                    own[:, at + d : at + 2 * d].astype(jnp.bfloat16),
+                ],
+                1,
+            )
+            grad_qkv = lax.optimization_barrier(grad_qkv)
+            grads.append(grad_qkv)
+            total, parts = reduce_rows(blocks, grad_qkv)
+            sums.append(parts)
+    grad_qkv = jnp.concatenate(grads, 1)
     if head_count == 2:
-        far_part = lax.ppermute(peer_part.astype(jnp.bfloat16), "head", [(0, 1), (1, 0)])
-        d_tokens = own_part + far_part.astype(jnp.float32)
+        peer_rows = lax.dynamic_slice_in_dim(grad_qkv, (1 - head_pos) * part_rows, part_rows, 0)
+        far_part = lax.ppermute(
+            dot_nt(peer_rows, weights).astype(jnp.bfloat16), "head", [(0, 1), (1, 0)]
+        )
+        far_part, _ = lax.optimization_barrier((far_part, total))
+        mine = lax.dynamic_slice_in_dim(grad_qkv, head_pos * part_rows, part_rows, 0)
+        d_tokens = dot_nt(mine, weights) + far_part.astype(jnp.float32)
     else:
-        d_tokens = lax.psum_scatter(own_part, "head", scatter_dimension=0, tiled=True)
+        d_tokens = lax.psum_scatter(
+            dot_nt(grad_qkv, weights), "head", scatter_dimension=0, tiled=True
+        )
     d_tokens = d_tokens.astype(jnp.bfloat16)
     attn_out = jnp.concatenate(outs, 1)
-    gradient = jnp.stack(sums, 1) / scale_power
-    first_new = beta_one * adam_first + (1.0 - beta_one) * gradient
-    second_new = beta_two * adam_second + (1.0 - beta_two) * gradient * gradient
-    first_fix = 1.0 - beta_one**ADAM_STEP
-    second_fix = 1.0 - beta_two**ADAM_STEP
-    update = first_new / first_fix / (jnp.sqrt(second_new / second_fix) + adam_eps)
-    master_new = qkv_master - learn_rate * (update + weight_decay * qkv_master)
     own_flags = lax.dynamic_slice_in_dim(skip_flag, head_pos * kv_groups, kv_groups, 0)
-    applied = (own_flags == 0)[None, :, None]
-    return (
-        attn_out,
-        d_tokens,
-        jnp.where(applied, master_new, qkv_master),
-        jnp.where(applied, first_new, adam_first),
-        jnp.where(applied, second_new, adam_second),
+    stepped = adam_step(
+        own_flags, (1.0 / scale_power).reshape(1), sums, qkv_master, adam_first, adam_second
     )
+    return (attn_out, d_tokens, *stepped)
 
 
 def solution(mesh):

time: 658 us -> 521 us (0.79)
  waiting for transfers between devices: 377 us -> 295 us
  local copies, waits for them, and re-layouts: 72.7 us -> 11.1 us
  Pallas kernels: 42.7 us -> 53.2 us
  other arithmetic: 12.9 us -> 20.6 us
  matrix products: 80.8 us -> 73.2 us
    unnamed x12 -> x1, waiting for transfers between devices: 183 us -> 0.02 us
    ppermute x1 -> x21, waiting for transfers between devices: 29.9 us -> 176 us  [the longest x4 102 us: reduce_rows(): got_chip = lax.ppermute(sent, 'seq', [(i, i ^ 2) for i in devices])]
    ppermute x16 -> x8, waiting for transfers between devices: 109 us -> 13.2 us  [shifted(): return lax.ppermute(block, axis, route)]
    unnamed x53 -> x32, local copies, waits for them, and re-layouts: 70.2 us -> 9.93 us
    all_gather x4 -> x1, waiting for transfers between devices: 56 us -> 105 us  [per_device(): weights = lax.all_gather(master16, 'seq', axis=0, tiled=True)]
    ppermute x1 -> x21, starting transfers between devices: 1.94 us -> 25.1 us  [the longest x12 17 us: reduce_rows(): got = lax.ppermute(part((outer_pos + step) % outer), 'seq', route)]
    dot_general x4 -> x0, matrix products: 22.7 us -> none  [per_device(): lax.dot_general(normed, grad_qkv, (((0,), (0,)), ((), ())), preferred_ele...]
    dot_general x4 -> x14, matrix products: 27.4 us -> 48.6 us  [dot_nn(): return jnp.dot(a, b, preferred_element_type=jnp.float32)]
  transfers between devices with their start and end apart: 25 -> 30, of which waited for: 21 -> 14; matrix products, arithmetic and copies ran while one was open for 21% -> 17% of each run, Pallas kernels for 7% -> 9%
where the time goes in v2:
time: 521 us; the launch traced here: 516 us
  waiting for transfers between devices  295 us (57%)
  matrix products  73.2 us (14%)
  Pallas kernels  53.2 us (10%)
  starting transfers between devices  47.5 us (9%)
  other arithmetic  20.6 us (4%)
  between operations  15.7 us (3%)
  local copies, waits for them, and re-layouts  11.1 us (2%)
    all_gather x1, waiting for transfers between devices, per_device(): weights = lax.all_gather(master16, 'seq', axis=0, tiled=True)  105 us
    ppermute x4, waiting for transfers between devices, reduce_rows(): got_chip = lax.ppermute(sent, 'seq', [(i, i ^ 2) for i in devices])  102 us
    ppermute x12, waiting for transfers between devices, reduce_rows(): got = lax.ppermute(part((outer_pos + step) % outer), 'seq', route)  74.4 us
    dot_general x14, matrix products, dot_nn(): return jnp.dot(a, b, preferred_element_type=jnp.float32)  48.6 us
    pallas_call x2, Pallas kernels, group_attention(): pl.pallas_call(functools.partial(attention_kernel, halo_span), grid=(grou...  43.9 us
    dot_general x2, matrix products, dot_nt(): lax.dot_general(a, b, (((1,), (1,)), ((), ())), preferred_element_type=jn...  24.6 us
    ppermute x8, starting transfers between devices, shifted(): return lax.ppermute(block, axis, route)  22.4 us
    ppermute x12, starting transfers between devices, reduce_rows(): got = lax.ppermute(part((outer_pos + step) % outer), 'seq', route)  17 us
  transfers between devices with their start and end apart: 30, of which 14 were waited for; matrix products, arithmetic and copies ran while one was open for 17% of the time, Pallas kernels for 9%

profile of v2, /device:TPU:8, one launch (start us, length us, event | category | flops | bytes accessed | tf_op | source)
XLA Modules:
  0.0 516.0 jit_solution(5403077746628574474)
XLA Ops:
  11.7 8.4 %copy.12 = bf16[512,5376]{0,1:T(8,128)(2,1)} copy(bf16[512,5376]{1,0:T(8,128)(2,1)} %param.7) | data formatting | bytes 11010048 | tf_op args[0]
  20.6 105.4 %all-gather.2.cloned.1.call-done = bf16[5376,2048]{1,0:T(8,128)(2,1)} async-done(((bf16[336,2048]{1,0:T(8,128)(2,1)}), bf16[5376,2048]{1,0:T(8,128)(2,1)}) %all-gather.2.cloned.1.call-update) | async-done | bytes 22020112 | tf_op jit(solution)/shard_map/all_gather | solution.py:274
  126.0 10.2 %fusion.18 = (bf16[512,1024]{1,0:T(8,128)(2,1)S(1)}, f32[512,1024]{1,0:T(8,128)S(1)}) fusion(bf16[512,5376]{1,0:T(8,128)(2,1)} %param.7, bf16[5376,2048]{1,0:T(8,128)(2,1)} %all-gather.2.cloned.1.call-done), kind=kOutput, calls=%fused_computation.88 | convolution fusion | flops 5637668864 | bytes 19660800 | tf_op jit(solution)/shard_map/dot_general | solution.py:49
  142.2 10.3 %fusion.19 = (bf16[512,1024]{1,0:T(8,128)(2,1)S(1)}, f32[512,1024]{1,0:T(8,128)S(1)}) fusion(bf16[512,5376]{1,0:T(8,128)(2,1)} %param.7, bf16[5376,2048]{1,0:T(8,128)(2,1)} %all-gather.2.cloned.1.call-done), kind=kOutput, calls=%fused_computation.89 | convolution fusion | flops 5637668864 | bytes 19660800 | tf_op jit(solution)/shard_map/dot_general | solution.py:49
  153.0 3.6 collective-permute-start
  160.4 21.9 %shard_map.111 = (bf16[512,512]{1,0:T(8,128)(2,1)S(1)}, bf16[512,512]{1,0:T(8,128)(2,1)S(1)}, f32[512,512]{1,0:T(8,128)S(1)}, bf16[512,512]{1,0:T(8,128)(2,1)S(1)}, bf16[512,512]{1,0:T(8,128)(2,1)S(1)}) custom-call(s32[1]{0:T(128)} %bitcast.start_ref, f32[512,1024]{1,0:T(8,128)S(1)} %get-tuple-element.88.qkv_ref, ...), custom_call_target="tpu_custom_call" | custom-call | flops 3019898880 | bytes 6291456 | tf_op jit(solution)/shard_map/pallas_call | solution.py:141
  182.3 3.6 collective-permute-start.7
  188.3 21.9 %shard_map.110 = (bf16[512,512]{1,0:T(8,128)(2,1)S(1)}, bf16[512,512]{1,0:T(8,128)(2,1)S(1)}, f32[512,512]{1,0:T(8,128)S(1)}, bf16[512,512]{1,0:T(8,128)(2,1)S(1)}, bf16[512,512]{1,0:T(8,128)(2,1)S(1)}) custom-call(s32[1]{0:T(128)} %bitcast.start_ref, f32[512,1024]{1,0:T(8,128)S(1)} %get-tuple-element.90.qkv_ref, ...), custom_call_target="tpu_custom_call" | custom-call | flops 3019898880 | bytes 6291456 | tf_op jit(solution)/shard_map/pallas_call | solution.py:141
  216.8 9.7 %collective-permute-done.5 = bf16[512,512]{1,0:T(8,128)(2,1)S(1)} collective-permute-done((bf16[512,512]{1,0:T(8,128)(2,1)S(1)}, bf16[512,512]{1,0:T(8,128)(2,1)S(1)}, u32[]{:S(2)}, u32[]{:S(2)}) %collective-permute-start.5) | collective-permute-done | bytes 524320 | tf_op jit(solution)/shard_map/ppermute | solution.py:31
  226.4 3.5 collective-permute-done.4
  240.9 12.1 %convolution_convert_fusion = bf16[256,5376]{1,0:T(8,128)(2,1)} fusion(bf16[5376,2048]{1,0:T(8,128)(2,1)} %all-gather.2.cloned.1.call-done, bf16[512,2048]{1,0:T(8,128)(2,1)} %pad_maximum_fusion.1, s32[]{:T(128)S(6)} %select_n.112), kind=kOutput, calls=%fused_computation.4 | convolution fusion | flops 5638520832 | bytes 25821188 | tf_op jit(solution)/shard_map/dot_general | solution.py:45
  266.0 12.5 %fusion.5 = f32[256,5376]{1,0:T(8,128)} fusion(bf16[5376,2048]{1,0:T(8,128)(2,1)} %all-gather.2.cloned.1.call-done, bf16[512,2048]{1,0:T(8,128)(2,1)} %pad_maximum_fusion.1, s32[]{:T(128)S(6)} %select_n.111), kind=kOutput, calls=%fused_computation.23 | convolution fusion | flops 5637144576 | bytes 28573700 | tf_op jit(solution)/shard_map/dot_general | solution.py:45
  293.5 20.3 %collective-permute-done.12 = bf16[1344,512]{1,0:T(8,128)(2,1)S(1)} collective-permute-done((bf16[1344,512]{1,0:T(8,128)(2,1)S(1)}, bf16[1344,512]{1,0:T(8,128)(2,1)S(1)}, u32[]{:S(2)}, u32[]{:S(2)}) %collective-permute-start.12) | collective-permute-done | bytes 1376288 | tf_op jit(solution)/shard_map/ppermute | solution.py:195
  317.5 25.8 %collective-permute-done.17 = bf16[1344,512]{1,0:T(8,128)(2,1)S(1)} collective-permute-done((bf16[1344,512]{1,0:T(8,128)(2,1)S(1)}, bf16[1344,512]{1,0:T(8,128)(2,1)S(1)}, u32[]{:S(2)}, u32[]{:S(2)}) %collective-permute-start.17) | collective-permute-done | bytes 1376288 | tf_op jit(solution)/shard_map/ppermute | solution.py:195
  346.2 55.5 %collective-permute-done.22 = bf16[1344,512]{1,0:T(8,128)(2,1)S(1)} collective-permute-done((bf16[1344,512]{1,0:T(8,128)(2,1)S(1)}, bf16[1344,512]{1,0:T(8,128)(2,1)S(1)}, u32[]{:S(2)}, u32[]{:S(2)}) %collective-permute-start.22) | collective-permute-done | bytes 1376288 | tf_op jit(solution)/shard_map/ppermute | solution.py:195
  412.8 13.6 %collective-permute-done.15.refs_3_ = bf16[336,512]{1,0:T(8,128)(2,1)S(1)} collective-permute-done((bf16[336,512]{1,0:T(8,128)(2,1)S(1)}, bf16[336,512]{1,0:T(8,128)(2,1)S(1)}, u32[]{:S(2)}, u32[]{:S(2)}) %collective-permute-start.15) | collective-permute-done | bytes 344096 | tf_op jit(solution)/shard_map/ppermute | solution.py:207
  426.9 14.2 %collective-permute-done.19.refs_6_ = bf16[336,512]{1,0:T(8,128)(2,1)S(1)} collective-permute-done((bf16[336,512]{1,0:T(8,128)(2,1)S(1)}, bf16[336,512]{1,0:T(8,128)(2,1)S(1)}, u32[]{:S(2)}, u32[]{:S(2)}) %collective-permute-start.19) | collective-permute-done | bytes 344096 | tf_op jit(solution)/shard_map/ppermute | solution.py:207
  441.1 6.5 %collective-permute-start.26 = (bf16[336,512]{1,0:T(8,128)(2,1)S(1)}, bf16[336,512]{1,0:T(8,128)(2,1)S(1)}, u32[]{:S(2)}, u32[]{:S(2)}) collective-permute-start(bf16[336,512]{1,0:T(8,128)(2,1)S(1)} %get-tuple-element.59), channel_id=1, source_target_pairs={{0,8},{2,10},{4,12},{6,14},{8,16},{10,18},{12,20},{14,22},{16,24},... | collective-permute-start | bytes 1032200 | tf_op jit(solution)/shard_map/ppermute | solution.py:207
  447.6 20.3 %collective-permute-done.20.refs_7_ = bf16[336,512]{1,0:T(8,128)(2,1)S(1)} collective-permute-done((bf16[336,512]{1,0:T(8,128)(2,1)S(1)}, bf16[336,512]{1,0:T(8,128)(2,1)S(1)}, u32[]{:S(2)}, u32[]{:S(2)}) %collective-permute-start.20) | collective-permute-done | bytes 344096 | tf_op jit(solution)/shard_map/ppermute | solution.py:207
  468.9 4.4 add_convert_fusion
  473.3 10.8 %collective-permute-done.24.refs_10_ = bf16[336,512]{1,0:T(8,128)(2,1)S(1)} collective-permute-done((bf16[336,512]{1,0:T(8,128)(2,1)S(1)}, bf16[336,512]{1,0:T(8,128)(2,1)S(1)}, u32[]{:S(2)}, u32[]{:S(2)}) %collective-permute-start.24) | collective-permute-done | bytes 344096 | tf_op jit(solution)/shard_map/ppermute | solution.py:207
  486.4 5.0 collective-permute-done.26.refs_13_
  491.4 7.3 %collective-permute-done.27.refs_14_ = bf16[336,512]{1,0:T(8,128)(2,1)S(1)} collective-permute-done((bf16[336,512]{1,0:T(8,128)(2,1)S(1)}, bf16[336,512]{1,0:T(8,128)(2,1)S(1)}, u32[]{:S(2)}, u32[]{:S(2)}) %collective-permute-start.27) | collective-permute-done | bytes 344096 | tf_op jit(solution)/shard_map/ppermute | solution.py:207
  499.6 9.3 %shard_map.112 = (f32[336,4,512]{2,1,0:T(4,128)}, f32[336,4,512]{2,1,0:T(4,128)}, f32[336,4,512]{2,1,0:T(4,128)}) custom-call(s32[4]{0:T(128)S(1)} %dynamic_slice.82.flag_ref, f32[1]{0:T(128)} %bitcast.10.scale_ref, bf16[336,512]{1,0:T(8,128)(2,1)S(1)} %get-tuple-element.72.refs_0_, bf16[336,512]{1,0:T(8,128)(2,1)S(1)} %collective-permute-done.13.refs_1_, ...), custom_call_target="tpu_custom_call" | custom-call | flops 13762560 | bytes 22020096 | tf_op jit(solution)/shard_map/pallas_call | solution.py:246
  (134 shorter events, 84.1 us)
Async XLA Ops:
  7.2 118.9 %all-gather.2.cloned.1.call-start = ((), (), s32[]{:S(2)}) async-start(), calls=%async_computation | async-start | bytes 23396352 | tf_op jit(solution)/shard_map/all_gather | solution.py:274
  153.0 35.2 %collective-permute-start = (bf16[512,512]{1,0:T(8,128)(2,1)S(1)}, bf16[512,512]{1,0:T(8,128)(2,1)S(1)}, u32[]{:S(2)}, u32[]{:S(2)}) collective-permute-start(bf16[512,512]{1,0:T(8,128)(2,1)S(1)} %pad_maximum_fusion.3.refs_2_), channel_id=1, source_target_pairs={{0,4},{2,6},{4,8},{6,10},{8,12},{10,14},{12,16},{14,18},{16,20},{1... | collective-permute-start | bytes 1572872 | tf_op jit(solution)/shard_map/ppermute | solution.py:31
  156.7 31.6 %collective-permute-start.1 = (bf16[512,512]{1,0:T(8,128)(2,1)S(1)}, bf16[512,512]{1,0:T(8,128)(2,1)S(1)}, u32[]{:S(2)}, u32[]{:S(2)}) collective-permute-start(bf16[512,512]{1,0:T(8,128)(2,1)S(1)} %pad_maximum_fusion.3.refs_2_), channel_id=1, source_target_pairs={{0,2},{2,4},{4,6},{6,8},{8,10},{10,12},{12,14},{14,16},{16,18},{18... | collective-permute-start | bytes 1572872 | tf_op jit(solution)/shard_map/ppermute | solution.py:31
  182.3 33.4 %collective-permute-start.7 = (bf16[512,512]{1,0:T(8,128)(2,1)S(1)}, bf16[512,512]{1,0:T(8,128)(2,1)S(1)}, u32[]{:S(2)}, u32[]{:S(2)}) collective-permute-start(bf16[512,512]{1,0:T(8,128)(2,1)S(1)} %get-tuple-element.28), channel_id=1, source_target_pairs={{4,0},{6,2},{8,4},{10,6},{12,8},{14,10},{16,12},{18,14},{20,16},{2... | collective-permute-start | bytes 1572872 | tf_op jit(solution)/shard_map/ppermute | solution.py:31
  185.9 29.8 %collective-permute-start.6 = (bf16[512,512]{1,0:T(8,128)(2,1)S(1)}, bf16[512,512]{1,0:T(8,128)(2,1)S(1)}, u32[]{:S(2)}, u32[]{:S(2)}) collective-permute-start(bf16[512,512]{1,0:T(8,128)(2,1)S(1)} %get-tuple-element.27), channel_id=1, source_target_pairs={{2,0},{4,2},{6,4},{8,6},{10,8},{12,10},{14,12},{16,14},{18,16},{20... | collective-permute-start | bytes 1572872 | tf_op jit(solution)/shard_map/ppermute | solution.py:31
  234.2 44.4 %collective-permute-start.11 = (bf16[2688,512]{1,0:T(8,128)(2,1)}, bf16[2688,512]{1,0:T(8,128)(2,1)}, u32[]{:S(2)}, u32[]{:S(2)}) collective-permute-start(bf16[2688,512]{1,0:T(8,128)(2,1)} %convolution_convert_fusion.3), channel_id=1, source_target_pairs={{0,2},{2,0},{4,6},{6,4},{8,10},{10,8},{12,14},{14,12},{16,18},{18,... | collective-permute-start | bytes 8257544 | tf_op jit(solution)/shard_map/ppermute | solution.py:193
  255.4 28.4 %collective-permute-start.16 = (bf16[2688,512]{1,0:T(8,128)(2,1)}, bf16[2688,512]{1,0:T(8,128)(2,1)}, u32[]{:S(2)}, u32[]{:S(2)}) collective-permute-start(bf16[2688,512]{1,0:T(8,128)(2,1)} %convolution_convert_fusion.2), channel_id=1, source_target_pairs={{0,2},{2,0},{4,6},{6,4},{8,10},{10,8},{12,14},{14,12},{16,18},{18,... | collective-permute-start | bytes 8257544 | tf_op jit(solution)/shard_map/ppermute | solution.py:193
  264.1 139.9 %collective-permute-start.8 = (bf16[256,5376]{1,0:T(8,128)(2,1)}, bf16[256,5376]{1,0:T(8,128)(2,1)}, u32[]{:S(2)}, u32[]{:S(2)}) collective-permute-start(bf16[256,5376]{1,0:T(8,128)(2,1)} %convolution_convert_fusion), channel_id=1, source_target_pairs={{0,1},{1,0},{2,3},{3,2},{4,5},{5,4},{6,7},{7,6},{8,9},{9,8},{10,11... | collective-permute-start | bytes 8257544 | tf_op jit(solution)/shard_map/ppermute | solution.py:313
  265.7 24.7 %collective-permute-start.21 = (bf16[2688,512]{1,0:T(8,128)(2,1)}, bf16[2688,512]{1,0:T(8,128)(2,1)}, u32[]{:S(2)}, u32[]{:S(2)}) collective-permute-start(bf16[2688,512]{1,0:T(8,128)(2,1)} %convolution_convert_fusion.1), channel_id=1, source_target_pairs={{0,2},{2,0},{4,6},{6,4},{8,10},{10,8},{12,14},{14,12},{16,18},{18,... | collective-permute-start | bytes 8257544 | tf_op jit(solution)/shard_map/ppermute | solution.py:193
  280.8 33.1 %collective-permute-start.12 = (bf16[1344,512]{1,0:T(8,128)(2,1)S(1)}, bf16[1344,512]{1,0:T(8,128)(2,1)S(1)}, u32[]{:S(2)}, u32[]{:S(2)}) collective-permute-start(bf16[1344,512]{1,0:T(8,128)(2,1)S(1)} %add_convert_fusion.6), channel_id=1, source_target_pairs={{0,4},{2,6},{4,0},{6,2},{8,12},{10,14},{12,8},{14,10},{16,20},{18,... | collective-permute-start | bytes 4128776 | tf_op jit(solution)/shard_map/ppermute | solution.py:195
  286.0 57.3 %collective-permute-start.17 = (bf16[1344,512]{1,0:T(8,128)(2,1)S(1)}, bf16[1344,512]{1,0:T(8,128)(2,1)S(1)}, u32[]{:S(2)}, u32[]{:S(2)}) collective-permute-start(bf16[1344,512]{1,0:T(8,128)(2,1)S(1)} %add_convert_fusion.4), channel_id=1, source_target_pairs={{0,4},{2,6},{4,0},{6,2},{8,12},{10,14},{12,8},{14,10},{16,20},{18,... | collective-permute-start | bytes 4128776 | tf_op jit(solution)/shard_map/ppermute | solution.py:195
  289.1 116.9 %collective-permute-start.10 = (bf16[1344,512]{1,0:T(8,128)(2,1)S(1)}, bf16[1344,512]{1,0:T(8,128)(2,1)S(1)}, u32[]{:S(2)}, u32[]{:S(2)}) collective-permute-start(bf16[1344,512]{1,0:T(8,128)(2,1)S(1)} %add_convert_fusion.8), channel_id=1, source_target_pairs={{0,4},{2,6},{4,0},{6,2},{8,12},{10,14},{12,8},{14,10},{16,20},{18,... | collective-permute-start | bytes 4128776 | tf_op jit(solution)/shard_map/ppermute | solution.py:195
  292.6 109.0 %collective-permute-start.22 = (bf16[1344,512]{1,0:T(8,128)(2,1)S(1)}, bf16[1344,512]{1,0:T(8,128)(2,1)S(1)}, u32[]{:S(2)}, u32[]{:S(2)}) collective-permute-start(bf16[1344,512]{1,0:T(8,128)(2,1)S(1)} %add_convert_fusion.2), channel_id=1, source_target_pairs={{0,4},{2,6},{4,0},{6,2},{8,12},{10,14},{12,8},{14,10},{16,20},{18,... | collective-permute-start | bytes 4128776 | tf_op jit(solution)/shard_map/ppermute | solution.py:195
  316.0 92.6 %collective-permute-start.13 = (bf16[336,512]{1,0:T(8,128)(2,1)S(1)}, bf16[336,512]{1,0:T(8,128)(2,1)S(1)}, u32[]{:S(2)}, u32[]{:S(2)}) collective-permute-start(bf16[336,512]{1,0:T(8,128)(2,1)S(1)} %get-tuple-element.71), channel_id=1, source_target_pairs={{0,8},{2,10},{4,12},{6,14},{8,16},{10,18},{12,20},{14,22},{16,24},... | collective-permute-start | bytes 1032200 | tf_op jit(solution)/shard_map/ppermute | solution.py:207
  343.3 65.6 %collective-permute-start.14 = (bf16[336,512]{1,0:T(8,128)(2,1)S(1)}, bf16[336,512]{1,0:T(8,128)(2,1)S(1)}, u32[]{:S(2)}, u32[]{:S(2)}) collective-permute-start(bf16[336,512]{1,0:T(8,128)(2,1)S(1)} %get-tuple-element.70), channel_id=1, source_target_pairs={{0,16},{2,18},{4,20},{6,22},{8,24},{10,26},{12,28},{14,30},{16,0},... | collective-permute-start | bytes 1032200 | tf_op jit(solution)/shard_map/ppermute | solution.py:207
  401.6 24.8 %collective-permute-start.15 = (bf16[336,512]{1,0:T(8,128)(2,1)S(1)}, bf16[336,512]{1,0:T(8,128)(2,1)S(1)}, u32[]{:S(2)}, u32[]{:S(2)}) collective-permute-start(bf16[336,512]{1,0:T(8,128)(2,1)S(1)} %get-tuple-element.69), channel_id=1, source_target_pairs={{0,24},{2,26},{4,28},{6,30},{8,0},{10,2},{12,4},{14,6},{16,8},{18,... | collective-permute-start | bytes 1032200 | tf_op jit(solution)/shard_map/ppermute | solution.py:207
  406.0 35.1 %collective-permute-start.19 = (bf16[336,512]{1,0:T(8,128)(2,1)S(1)}, bf16[336,512]{1,0:T(8,128)(2,1)S(1)}, u32[]{:S(2)}, u32[]{:S(2)}) collective-permute-start(bf16[336,512]{1,0:T(8,128)(2,1)S(1)} %get-tuple-element.66), channel_id=1, source_target_pairs={{0,16},{2,18},{4,20},{6,22},{8,24},{10,26},{12,28},{14,30},{16,0},... | collective-permute-start | bytes 1032200 | tf_op jit(solution)/shard_map/ppermute | solution.py:207
  408.6 59.4 %collective-permute-start.20 = (bf16[336,512]{1,0:T(8,128)(2,1)S(1)}, bf16[336,512]{1,0:T(8,128)(2,1)S(1)}, u32[]{:S(2)}, u32[]{:S(2)}) collective-permute-start(bf16[336,512]{1,0:T(8,128)(2,1)S(1)} %get-tuple-element.65), channel_id=1, source_target_pairs={{0,24},{2,26},{4,28},{6,30},{8,0},{10,2},{12,4},{14,6},{16,8},{18,... | collective-permute-start | bytes 1032200 | tf_op jit(solution)/shard_map/ppermute | solution.py:207
  408.9 59.0 %collective-permute-start.23 = (bf16[336,512]{1,0:T(8,128)(2,1)S(1)}, bf16[336,512]{1,0:T(8,128)(2,1)S(1)}, u32[]{:S(2)}, u32[]{:S(2)}) collective-permute-start(bf16[336,512]{1,0:T(8,128)(2,1)S(1)} %get-tuple-element.63), channel_id=1, source_target_pairs={{0,8},{2,10},{4,12},{6,14},{8,16},{10,18},{12,20},{14,22},{16,24},... | collective-permute-start | bytes 1032200 | tf_op jit(solution)/shard_map/ppermute | solution.py:207
  426.4 57.6 %collective-permute-start.24 = (bf16[336,512]{1,0:T(8,128)(2,1)S(1)}, bf16[336,512]{1,0:T(8,128)(2,1)S(1)}, u32[]{:S(2)}, u32[]{:S(2)}) collective-permute-start(bf16[336,512]{1,0:T(8,128)(2,1)S(1)} %get-tuple-element.62), channel_id=1, source_target_pairs={{0,16},{2,18},{4,20},{6,22},{8,24},{10,26},{12,28},{14,30},{16,0},... | collective-permute-start | bytes 1032200 | tf_op jit(solution)/shard_map/ppermute | solution.py:207
  426.4 60.0 %collective-permute-start.25 = (bf16[336,512]{1,0:T(8,128)(2,1)S(1)}, bf16[336,512]{1,0:T(8,128)(2,1)S(1)}, u32[]{:S(2)}, u32[]{:S(2)}) collective-permute-start(bf16[336,512]{1,0:T(8,128)(2,1)S(1)} %get-tuple-element.61), channel_id=1, source_target_pairs={{0,24},{2,26},{4,28},{6,30},{8,0},{10,2},{12,4},{14,6},{16,8},{18,... | collective-permute-start | bytes 1032200 | tf_op jit(solution)/shard_map/ppermute | solution.py:207
  441.1 50.3 %collective-permute-start.26 = (bf16[336,512]{1,0:T(8,128)(2,1)S(1)}, bf16[336,512]{1,0:T(8,128)(2,1)S(1)}, u32[]{:S(2)}, u32[]{:S(2)}) collective-permute-start(bf16[336,512]{1,0:T(8,128)(2,1)S(1)} %get-tuple-element.59), channel_id=1, source_target_pairs={{0,8},{2,10},{4,12},{6,14},{8,16},{10,18},{12,20},{14,22},{16,24},... | collective-permute-start | bytes 1032200 | tf_op jit(solution)/shard_map/ppermute | solution.py:207
  468.0 30.7 %collective-permute-start.27 = (bf16[336,512]{1,0:T(8,128)(2,1)S(1)}, bf16[336,512]{1,0:T(8,128)(2,1)S(1)}, u32[]{:S(2)}, u32[]{:S(2)}) collective-permute-start(bf16[336,512]{1,0:T(8,128)(2,1)S(1)} %get-tuple-element.58), channel_id=1, source_target_pairs={{0,16},{2,18},{4,20},{6,22},{8,24},{10,26},{12,28},{14,30},{16,0},... | collective-permute-start | bytes 1032200 | tf_op jit(solution)/shard_map/ppermute | solution.py:207
  468.0 31.6 %collective-permute-start.28 = (bf16[336,512]{1,0:T(8,128)(2,1)S(1)}, bf16[336,512]{1,0:T(8,128)(2,1)S(1)}, u32[]{:S(2)}, u32[]{:S(2)}) collective-permute-start(bf16[336,512]{1,0:T(8,128)(2,1)S(1)} %get-tuple-element.57), channel_id=1, source_target_pairs={{0,24},{2,26},{4,28},{6,30},{8,0},{10,2},{12,4},{14,6},{16,8},{18,... | collective-permute-start | bytes 1032200 | tf_op jit(solution)/shard_map/ppermute | solution.py:207
  (21 other events, 595.6 us)
Sparse Core Ops, SparseCore 0:
  11.1 114.9 all-gather.1

commit v3 on v2

--- a/solution.py
+++ b/solution.py
@@ -182,7 +182,11 @@
     return other_core, pick(1 - mid, core), pick(mid, core)
 
 
-def reduce_rows(blocks, grad_qkv):
+def after(value, *earlier):
+    return lax.optimization_barrier((value, *earlier))[0]
+
+
+def reduce_rows(blocks, grad_qkv, earlier):
     other_core, other_chip, here = blocks
     seq_size = lax.axis_size("seq")
     outer_pos = lax.axis_index("seq") // 4
@@ -193,6 +197,7 @@
     got = lax.ppermute(sent, "seq", [(i, i ^ 1) for i in devices])
     sent = (dot_nn(other_chip, grad_qkv) + got[:half].astype(jnp.float32)).astype(jnp.bfloat16)
     got_chip = lax.ppermute(sent, "seq", [(i, i ^ 2) for i in devices])
+    got_chip = after(got_chip, *earlier)
     total = (
         dot_nn(here, grad_qkv) + got[half:].astype(jnp.float32) + got_chip.astype(jnp.float32)
     ).astype(jnp.bfloat16)
@@ -206,7 +211,7 @@
         route = [(i, (i + 4 * step) % seq_size) for i in devices]
         got = lax.ppermute(part((outer_pos + step) % outer), "seq", route)
         parts.append(got)
-    return total, parts
+    return sent, total, parts
 
 
 def adam_kernel(part_count, flag_ref, scale_ref, *refs):
@@ -271,12 +276,20 @@
     grad_out = (cotangent.astype(jnp.float32) * scale_power).astype(jnp.bfloat16)
 
     master16 = qkv_master.astype(jnp.bfloat16).reshape(own_rows, kv_groups * group_cols)
-    weights = lax.all_gather(master16, "seq", axis=0, tiled=True)
+    pair = 2 if kv_groups % 2 == 0 else 1
+    pair_cols = pair * group_cols
+    weights = [
+        lax.all_gather(master16[:, at : at + pair_cols], "seq", axis=0, tiled=True)
+        for at in range(0, kv_groups * group_cols, pair_cols)
+    ]
     blocks = row_blocks(normed, own_rows)
-    pair = 2 if kv_groups % 2 == 0 else 1
     outs, grads, sums = [], [], []
+    all_sent, totals = [], []
     for low in range(0, kv_groups, pair):
-        qkv = dot_nn(normed, weights[:, low * group_cols : (low + pair) * group_cols])
+        pair_weights = weights[low // pair]
+        if low:
+            pair_weights = after(pair_weights, *all_sent)
+        qkv = dot_nn(normed, pair_weights)
         kv, k_saved = [], []
         for g in range(pair):
             at = g * group_cols + q_cols
@@ -291,7 +304,11 @@
         )
         outs.append(out)
         for s in range(1, halo_span + 1):
-            own = own + shifted(backs[s - 1], "seq", -s).astype(jnp.float32)
+            back = shifted(backs[s - 1], "seq", -s)
+            if low:
+                back = after(back, *totals)
+            own = own + back.astype(jnp.float32)
+        pair_sent, pair_totals = [], []
         for g in range(pair):
             at = g * 2 * d
             gk = norm_back(*k_saved[g], own[:, at : at + d])
@@ -305,20 +322,30 @@
             )
             grad_qkv = lax.optimization_barrier(grad_qkv)
             grads.append(grad_qkv)
-            total, parts = reduce_rows(blocks, grad_qkv)
+            earlier = sums[-2] if len(sums) >= 2 else ()
+            sent, total, parts = reduce_rows(blocks, grad_qkv, earlier)
+            pair_sent.append(sent)
+            pair_totals.append(total)
             sums.append(parts)
-    grad_qkv = jnp.concatenate(grads, 1)
+        all_sent, totals = all_sent + pair_sent, totals + pair_totals
+
+    def token_terms(rows_at, row_count, *earlier):
+        terms = 0.0
+        for low in range(0, kv_groups, pair):
+            rows = jnp.concatenate(grads[low : low + pair], 1)
+            rows = lax.dynamic_slice_in_dim(after(rows, *earlier), rows_at, row_count, 0)
+            terms = terms + dot_nt(rows, weights[low // pair])
+        return terms
+
     if head_count == 2:
-        peer_rows = lax.dynamic_slice_in_dim(grad_qkv, (1 - head_pos) * part_rows, part_rows, 0)
-        far_part = lax.ppermute(
-            dot_nt(peer_rows, weights).astype(jnp.bfloat16), "head", [(0, 1), (1, 0)]
-        )
-        far_part, _ = lax.optimization_barrier((far_part, total))
-        mine = lax.dynamic_slice_in_dim(grad_qkv, head_pos * part_rows, part_rows, 0)
-        d_tokens = dot_nt(mine, weights) + far_part.astype(jnp.float32)
+        peer_terms = token_terms((1 - head_pos) * part_rows, part_rows, *all_sent)
+        far_part = lax.ppermute(peer_terms.astype(jnp.bfloat16), "head", [(0, 1), (1, 0)])
+        far_part = after(far_part, total)
+        d_tokens = token_terms(head_pos * part_rows, part_rows, total)
+        d_tokens = d_tokens + far_part.astype(jnp.float32)
     else:
         d_tokens = lax.psum_scatter(
-            dot_nt(grad_qkv, weights), "head", scatter_dimension=0, tiled=True
+            token_terms(0, tok_rows), "head", scatter_dimension=0, tiled=True
         )
     d_tokens = d_tokens.astype(jnp.bfloat16)
     attn_out = jnp.concatenate(outs, 1)

time: 521 us -> 536 us (1.029)
  waiting for transfers between devices: 295 us -> 257 us
  matrix products: 73.2 us -> 96.7 us
  local copies, waits for them, and re-layouts: 11.1 us -> 27.8 us
    ppermute x8, waiting for transfers between devices: 13.2 us -> 121 us  [shifted(): return lax.ppermute(block, axis, route)]
    ppermute x4, waiting for transfers between devices: 102 us -> 0.01 us  [reduce_rows(): got_chip = lax.ppermute(sent, 'seq', [(i, i ^ 2) for i in devices])]
    ppermute x12, waiting for transfers between devices: 74.4 us -> 42.7 us  [reduce_rows(): got = lax.ppermute(part((outer_pos + step) % outer), 'seq', route)]
    dot_general x2 -> x4, matrix products: 24.6 us -> 51 us  [dot_nt(): lax.dot_general(a, b, (((1,), (1,)), ((), ())), preferred_element_type=jn...]
    all_gather x1 -> x2, waiting for transfers between devices: 105 us -> 89.9 us  [per_device(): lax.all_gather(master16[:, at:at + pair_cols], 'seq', axis=0, tiled=True)]
    unnamed x32 -> x82, local copies, waits for them, and re-layouts: 9.93 us -> 17.5 us
  transfers between devices with their start and end apart: 30 -> 31, of which waited for: 14 -> 13; matrix products, arithmetic and copies ran while one was open for 17% -> 24% of each run, Pallas kernels for 9% -> 10%
where the time goes in v3:
time: 536 us; the launch traced here: 527 us
  waiting for transfers between devices  257 us (48%)
  matrix products  96.7 us (18%)
  Pallas kernels  54.6 us (10%)
  starting transfers between devices  51.1 us (10%)
  local copies, waits for them, and re-layouts  27.8 us (5%)
  other arithmetic  23.3 us (4%)
  between operations  16 us (3%)
    ppermute x8, waiting for transfers between devices, shifted(): return lax.ppermute(block, axis, route)  121 us
    all_gather x2, waiting for transfers between devices, per_device(): lax.all_gather(master16[:, at:at + pair_cols], 'seq', axis=0, tiled=True)  89.9 us
    dot_general x4, matrix products, dot_nt(): lax.dot_general(a, b, (((1,), (1,)), ((), ())), preferred_element_type=jn...  51 us
    dot_general x14, matrix products, dot_nn(): return jnp.dot(a, b, preferred_element_type=jnp.float32)  45.7 us
    pallas_call x2, Pallas kernels, group_attention(): pl.pallas_call(functools.partial(attention_kernel, halo_span), grid=(grou...  44.5 us
    ppermute x12, waiting for transfers between devices, reduce_rows(): got = lax.ppermute(part((outer_pos + step) % outer), 'seq', route)  42.7 us
    ppermute x8, starting transfers between devices, shifted(): return lax.ppermute(block, axis, route)  24.1 us
    unnamed x82, local copies, waits for them, and re-layouts  17.5 us
  transfers between devices with their start and end apart: 31, of which 13 were waited for; matrix products, arithmetic and copies ran while one was open for 24% of the time, Pallas kernels for 10%

profile of v3, /device:TPU:8, one launch (start us, length us, event | category | flops | bytes accessed | tf_op | source)
XLA Modules:
  0.0 526.5 jit_solution(10689432867920083437)
XLA Ops:
  12.5 89.9 %all-gather.3.cloned.1.call-done = bf16[5376,1024]{1,0:T(8,128)(2,1)} async-done(((bf16[336,1024]{1,0:T(8,128)(2,1)}), bf16[5376,1024]{1,0:T(8,128)(2,1)}) %all-gather.3.cloned.1.call-update) | async-done | bytes 11010064 | tf_op jit(solution)/shard_map/all_gather | solution.py:282
  102.4 10.2 %fusion.21 = (bf16[512,1024]{1,0:T(8,128)(2,1)S(1)}, f32[512,1024]{1,0:T(8,128)S(1)}) fusion(bf16[512,5376]{1,0:T(8,128)(2,1)} %param.7, bf16[5376,1024]{1,0:T(8,128)(2,1)} %all-gather.3.cloned.1.call-done), kind=kOutput, calls=%fused_computation.94 | convolution fusion | flops 5637668864 | bytes 19660800 | tf_op jit(solution)/shard_map/dot_general | solution.py:49
  118.7 23.3 %collective-permute-done.refs_0_ = bf16[512,512]{1,0:T(8,128)(2,1)S(1)} collective-permute-done((bf16[512,512]{1,0:T(8,128)(2,1)S(1)}, bf16[512,512]{1,0:T(8,128)(2,1)S(1)}, u32[]{:S(2)}, u32[]{:S(2)}) %collective-permute-start) | collective-permute-done | bytes 524320 | tf_op jit(solution)/shard_map/ppermute | solution.py:31
  142.0 12.1 %collective-permute-done.1.refs_1_ = bf16[512,512]{1,0:T(8,128)(2,1)S(1)} collective-permute-done((bf16[512,512]{1,0:T(8,128)(2,1)S(1)}, bf16[512,512]{1,0:T(8,128)(2,1)S(1)}, u32[]{:S(2)}, u32[]{:S(2)}) %collective-permute-start.1) | collective-permute-done | bytes 524320 | tf_op jit(solution)/shard_map/ppermute | solution.py:31
  154.1 22.6 %shard_map.110 = (bf16[512,512]{1,0:T(8,128)(2,1)S(1)}, bf16[512,512]{1,0:T(8,128)(2,1)S(1)}, f32[512,512]{1,0:T(8,128)S(1)}, bf16[512,512]{1,0:T(8,128)(2,1)}, bf16[512,512]{1,0:T(8,128)(2,1)}) custom-call(s32[1]{0:T(128)} %bitcast.start_ref, f32[512,1024]{1,0:T(8,128)S(1)} %get-tuple-element.108.qkv_ref, ...), custom_call_target="tpu_custom_call" | custom-call | flops 3019898880 | bytes 6291456 | tf_op jit(solution)/shard_map/pallas_call | solution.py:141
  182.7 8.3 %copy.13 = bf16[512,5376]{0,1:T(8,128)(2,1)} copy(bf16[512,5376]{1,0:T(8,128)(2,1)} %param.7) | data formatting | bytes 11010048 | tf_op args[0]
  191.0 4.3 constant_dynamic-slice_fusion
  196.2 21.6 %collective-permute-done.3 = bf16[512,512]{1,0:T(8,128)(2,1)} collective-permute-done((bf16[512,512]{1,0:T(8,128)(2,1)}, bf16[512,512]{1,0:T(8,128)(2,1)}, u32[]{:S(2)}, u32[]{:S(2)}) %collective-permute-start.3) | collective-permute-done | bytes 524320 | tf_op jit(solution)/shard_map/ppermute | solution.py:31
  228.7 3.4 collective-permute-start.10
  236.0 10.2 %fusion.22 = (bf16[512,1024]{1,0:T(8,128)(2,1)S(1)}, f32[512,1024]{1,0:T(8,128)S(1)}) fusion(bf16[512,5376]{1,0:T(8,128)(2,1)} %param.7, bf16[5376,1024]{1,0:T(8,128)(2,1)} %all-gather.5.cloned.1.call-done), kind=kOutput, calls=%fused_computation.95 | convolution fusion | flops 5637668864 | bytes 19660800 | tf_op jit(solution)/shard_map/dot_general | solution.py:49
  252.7 50.8 %collective-permute-done.6.refs_0_ = bf16[512,512]{1,0:T(8,128)(2,1)S(1)} collective-permute-done((bf16[512,512]{1,0:T(8,128)(2,1)S(1)}, bf16[512,512]{1,0:T(8,128)(2,1)S(1)}, u32[]{:S(2)}, u32[]{:S(2)}) %collective-permute-start.6) | collective-permute-done | bytes 524320 | tf_op jit(solution)/shard_map/ppermute | solution.py:31
  303.6 21.9 %shard_map.111 = (bf16[512,512]{1,0:T(8,128)(2,1)S(1)}, bf16[512,512]{1,0:T(8,128)(2,1)S(1)}, f32[512,512]{1,0:T(8,128)S(1)}, bf16[512,512]{1,0:T(8,128)(2,1)S(1)}, bf16[512,512]{1,0:T(8,128)(2,1)S(1)}) custom-call(s32[1]{0:T(128)} %bitcast.start_ref, f32[512,1024]{1,0:T(8,128)S(1)} %get-tuple-element.110.qkv_ref, ...), custom_call_target="tpu_custom_call" | custom-call | flops 3019898880 | bytes 6291456 | tf_op jit(solution)/shard_map/pallas_call | solution.py:141
  328.0 8.8 %collective-permute-start.11 = (bf16[512,512]{1,0:T(8,128)(2,1)S(1)}, bf16[512,512]{1,0:T(8,128)(2,1)S(1)}, u32[]{:S(2)}, u32[]{:S(2)}) collective-permute-start(bf16[512,512]{1,0:T(8,128)(2,1)S(1)} %get-tuple-element.39), channel_id=1, source_target_pairs={{4,0},{6,2},{8,4},{10,6},{12,8},{14,10},{16,12},{18,14},{20,16},{2... | collective-permute-start | bytes 1572872 | tf_op jit(solution)/shard_map/ppermute | solution.py:31
  341.0 12.1 %collective-permute-done.11 = bf16[512,512]{1,0:T(8,128)(2,1)S(1)} collective-permute-done((bf16[512,512]{1,0:T(8,128)(2,1)S(1)}, bf16[512,512]{1,0:T(8,128)(2,1)S(1)}, u32[]{:S(2)}, u32[]{:S(2)}) %collective-permute-start.11) | collective-permute-done | bytes 524320 | tf_op jit(solution)/shard_map/ppermute | solution.py:31
  383.2 13.0 %fusion.2 = f32[256,5376]{1,0:T(8,128)} fusion(bf16[5376,1024]{1,0:T(8,128)(2,1)} %all-gather.3.cloned.1.call-done, bf16[512,1024]{1,0:T(8,128)(2,1)S(1)} %pad_maximum_fusion.2, s32[]{:T(128)S(6)} %select_n.133), kind=kOutput, calls=%fused_computation.31 | convolution fusion | flops 2818572288 | bytes 17039364 | tf_op jit(solution)/shard_map/dot_general | solution.py:45
  396.2 13.4 %fusion = bf16[256,5376]{1,0:T(8,128)(2,1)} fusion(f32[256,5376]{1,0:T(8,128)} %fusion.2, bf16[5376,1024]{1,0:T(8,128)(2,1)} %all-gather.5.cloned.1.call-done, bf16[512,1024]{1,0:T(8,128)(2,1)S(1)} %copy-done.34, s32[]{:T(128)S(6)} %select_n.133), kind=kOutput, calls=%fused_computation.2 | convolution fusion | flops 2821324800 | bytes 19791876 | tf_op jit(solution)/shard_map/dot_general | solution.py:45
  419.2 16.0 %collective-permute-done.14.refs_5_ = bf16[336,512]{1,0:T(8,128)(2,1)S(1)} collective-permute-done((bf16[336,512]{1,0:T(8,128)(2,1)}, bf16[336,512]{1,0:T(8,128)(2,1)S(1)}, u32[]{:S(2)}, u32[]{:S(2)}) %collective-permute-start.14) | collective-permute-done | bytes 344096 | tf_op jit(solution)/shard_map/ppermute | solution.py:212
  437.7 16.1 %collective-permute-done.15.refs_6_ = bf16[336,512]{1,0:T(8,128)(2,1)S(1)} collective-permute-done((bf16[336,512]{1,0:T(8,128)(2,1)}, bf16[336,512]{1,0:T(8,128)(2,1)S(1)}, u32[]{:S(2)}, u32[]{:S(2)}) %collective-permute-start.15) | collective-permute-done | bytes 344096 | tf_op jit(solution)/shard_map/ppermute | solution.py:212
  462.7 13.0 %fusion.5 = f32[256,5376]{1,0:T(8,128)} fusion(bf16[5376,1024]{1,0:T(8,128)(2,1)} %all-gather.3.cloned.1.call-done, bf16[512,1024]{1,0:T(8,128)(2,1)S(1)} %copy-done.33, s32[]{:T(128)S(6)} %select_n.132), kind=kOutput, calls=%fused_computation.34 | convolution fusion | flops 2818572288 | bytes 17039364 | tf_op jit(solution)/shard_map/dot_general | solution.py:45
  479.1 11.5 %convolution_add_fusion.1 = f32[256,5376]{1,0:T(8,128)} fusion(f32[256,5376]{1,0:T(8,128)} %fusion.5, bf16[5376,1024]{1,0:T(8,128)(2,1)} %all-gather.5.cloned.1.call-done, bf16[512,1024]{1,0:T(8,128)(2,1)} %pad_maximum_fusion.3, s32[]{:T(128)S(6)} %select_n.132), kind=kOutput, calls=%fused_computation.1 | convolution fusion | flops 2819948544 | bytes 22544388 | tf_op jit(solution)/shard_map/dot_general | solution.py:45
  490.6 3.7 collective-permute-done.26.refs_13_
  494.3 4.9 collective-permute-done.27.refs_14_
  505.2 10.1 %shard_map.112 = (f32[336,4,512]{2,1,0:T(4,128)}, f32[336,4,512]{2,1,0:T(4,128)}, f32[336,4,512]{2,1,0:T(4,128)}) custom-call(s32[4]{0:T(128)S(1)} %dynamic_slice.94.flag_ref, f32[1]{0:T(128)} %bitcast.17.scale_ref, bf16[336,512]{1,0:T(8,128)(2,1)S(1)} %get-tuple-element.86.refs_0_, bf16[336,512]{1,0:T(8,128)(2,1)S(1)} %collective-permute-done.19.refs_1_, ...), custom_call_target="tpu_custom_call" | custom-call | flops 13762560 | bytes 22020096 | tf_op jit(solution)/shard_map/pallas_call | solution.py:251
  515.3 3.9 add_convert_fusion
  (190 shorter events, 105.3 us)
Async XLA Ops:
  7.2 95.2 %all-gather.3.cloned.1.call-start = ((), (), s32[]{:S(2)}) async-start(), calls=%async_computation | async-start | bytes 11698176 | tf_op jit(solution)/shard_map/all_gather | solution.py:282
  11.1 224.9 %all-gather.5.cloned.1.call-start = ((), (), s32[]{:S(2)}) async-start(), calls=%async_computation.1 | async-start | bytes 11698176 | tf_op jit(solution)/shard_map/all_gather | solution.py:282
  113.2 28.8 %collective-permute-start = (bf16[512,512]{1,0:T(8,128)(2,1)S(1)}, bf16[512,512]{1,0:T(8,128)(2,1)S(1)}, u32[]{:S(2)}, u32[]{:S(2)}) collective-permute-start(bf16[512,512]{1,0:T(8,128)(2,1)S(1)} %pad_maximum_fusion.4.refs_2_), channel_id=1, source_target_pairs={{0,4},{2,6},{4,8},{6,10},{8,12},{10,14},{12,16},{14,18},{16,20},{1... | collective-permute-start | bytes 1572872 | tf_op jit(solution)/shard_map/ppermute | solution.py:31
  115.7 38.4 %collective-permute-start.1 = (bf16[512,512]{1,0:T(8,128)(2,1)S(1)}, bf16[512,512]{1,0:T(8,128)(2,1)S(1)}, u32[]{:S(2)}, u32[]{:S(2)}) collective-permute-start(bf16[512,512]{1,0:T(8,128)(2,1)S(1)} %pad_maximum_fusion.4.refs_2_), channel_id=1, source_target_pairs={{0,2},{2,4},{4,6},{6,8},{8,10},{10,12},{12,14},{14,16},{16,18},{18... | collective-permute-start | bytes 1572872 | tf_op jit(solution)/shard_map/ppermute | solution.py:31
  180.3 37.5 %collective-permute-start.3 = (bf16[512,512]{1,0:T(8,128)(2,1)}, bf16[512,512]{1,0:T(8,128)(2,1)}, u32[]{:S(2)}, u32[]{:S(2)}) collective-permute-start(bf16[512,512]{1,0:T(8,128)(2,1)} %get-tuple-element.32), channel_id=1, source_target_pairs={{4,0},{6,2},{8,4},{10,6},{12,8},{14,10},{16,12},{18,14},{20,16},{2... | collective-permute-start | bytes 1572872 | tf_op jit(solution)/shard_map/ppermute | solution.py:31
  228.7 108.2 %collective-permute-start.10 = (bf16[1344,512]{1,0:T(8,128)(2,1)}, bf16[1344,512]{1,0:T(8,128)(2,1)S(1)}, u32[]{:S(2)}, u32[]{:S(2)}) collective-permute-start(bf16[1344,512]{1,0:T(8,128)(2,1)} %add_convert_fusion.7), channel_id=1, source_target_pairs={{0,4},{2,6},{4,0},{6,2},{8,12},{10,14},{12,8},{14,10},{16,20},{18,... | collective-permute-start | bytes 4128776 | tf_op jit(solution)/shard_map/ppermute | solution.py:199
  234.1 102.8 %collective-permute-start.9 = (bf16[1344,512]{1,0:T(8,128)(2,1)}, bf16[1344,512]{1,0:T(8,128)(2,1)}, u32[]{:S(2)}, u32[]{:S(2)}) collective-permute-start(bf16[1344,512]{1,0:T(8,128)(2,1)} %add_convert_fusion.8), channel_id=1, source_target_pairs={{0,4},{2,6},{4,0},{6,2},{8,12},{10,14},{12,8},{14,10},{16,20},{18,... | collective-permute-start | bytes 4128776 | tf_op jit(solution)/shard_map/ppermute | solution.py:199
  246.8 56.8 %collective-permute-start.6 = (bf16[512,512]{1,0:T(8,128)(2,1)S(1)}, bf16[512,512]{1,0:T(8,128)(2,1)S(1)}, u32[]{:S(2)}, u32[]{:S(2)}) collective-permute-start(bf16[512,512]{1,0:T(8,128)(2,1)S(1)} %pad_maximum_fusion.7.refs_2_), channel_id=1, source_target_pairs={{0,4},{2,6},{4,8},{6,10},{8,12},{10,14},{12,16},{14,18},{16,20},{1... | collective-permute-start | bytes 1572872 | tf_op jit(solution)/shard_map/ppermute | solution.py:31
  248.9 54.7 %collective-permute-start.7 = (bf16[512,512]{1,0:T(8,128)(2,1)S(1)}, bf16[512,512]{1,0:T(8,128)(2,1)S(1)}, u32[]{:S(2)}, u32[]{:S(2)}) collective-permute-start(bf16[512,512]{1,0:T(8,128)(2,1)S(1)} %pad_maximum_fusion.7.refs_2_), channel_id=1, source_target_pairs={{0,2},{2,4},{4,6},{6,8},{8,10},{10,12},{12,14},{14,16},{16,18},{18... | collective-permute-start | bytes 1572872 | tf_op jit(solution)/shard_map/ppermute | solution.py:31
  328.0 25.1 %collective-permute-start.11 = (bf16[512,512]{1,0:T(8,128)(2,1)S(1)}, bf16[512,512]{1,0:T(8,128)(2,1)S(1)}, u32[]{:S(2)}, u32[]{:S(2)}) collective-permute-start(bf16[512,512]{1,0:T(8,128)(2,1)S(1)} %get-tuple-element.39), channel_id=1, source_target_pairs={{4,0},{6,2},{8,4},{10,6},{12,8},{14,10},{16,12},{18,14},{20,16},{2... | collective-permute-start | bytes 1572872 | tf_op jit(solution)/shard_map/ppermute | solution.py:31
  365.4 44.2 %collective-permute-start.19 = (bf16[336,512]{1,0:T(8,128)(2,1)S(1)}, bf16[336,512]{1,0:T(8,128)(2,1)S(1)}, u32[]{:S(2)}, u32[]{:S(2)}) collective-permute-start(bf16[336,512]{1,0:T(8,128)(2,1)S(1)} %get-tuple-element.85), channel_id=1, source_target_pairs={{0,8},{2,10},{4,12},{6,14},{8,16},{10,18},{12,20},{14,22},{16,24},... | collective-permute-start | bytes 1032200 | tf_op jit(solution)/shard_map/ppermute | solution.py:212
  365.4 46.3 %collective-permute-start.20 = (bf16[336,512]{1,0:T(8,128)(2,1)}, bf16[336,512]{1,0:T(8,128)(2,1)S(1)}, u32[]{:S(2)}, u32[]{:S(2)}) collective-permute-start(bf16[336,512]{1,0:T(8,128)(2,1)} %get-tuple-element.84), channel_id=1, source_target_pairs={{0,16},{2,18},{4,20},{6,22},{8,24},{10,26},{12,28},{14,30},{16,0},... | collective-permute-start | bytes 1032200 | tf_op jit(solution)/shard_map/ppermute | solution.py:212
  368.4 45.1 %collective-permute-start.21 = (bf16[336,512]{1,0:T(8,128)(2,1)}, bf16[336,512]{1,0:T(8,128)(2,1)S(1)}, u32[]{:S(2)}, u32[]{:S(2)}) collective-permute-start(bf16[336,512]{1,0:T(8,128)(2,1)} %get-tuple-element.83), channel_id=1, source_target_pairs={{0,24},{2,26},{4,28},{6,30},{8,0},{10,2},{12,4},{14,6},{16,8},{18,... | collective-permute-start | bytes 1032200 | tf_op jit(solution)/shard_map/ppermute | solution.py:212
  377.9 35.9 %collective-permute-start.22 = (bf16[1344,512]{1,0:T(8,128)(2,1)}, bf16[1344,512]{1,0:T(8,128)(2,1)}, u32[]{:S(2)}, u32[]{:S(2)}) collective-permute-start(bf16[1344,512]{1,0:T(8,128)(2,1)} %add_convert_fusion.2), channel_id=1, source_target_pairs={{0,4},{2,6},{4,0},{6,2},{8,12},{10,14},{12,8},{14,10},{16,20},{18,... | collective-permute-start | bytes 4128776 | tf_op jit(solution)/shard_map/ppermute | solution.py:199
  381.2 75.8 %collective-permute-start.13 = (bf16[1344,512]{1,0:T(8,128)(2,1)}, bf16[1344,512]{1,0:T(8,128)(2,1)}, u32[]{:S(2)}, u32[]{:S(2)}) collective-permute-start(bf16[1344,512]{1,0:T(8,128)(2,1)} %add_convert_fusion.4), channel_id=1, source_target_pairs={{0,4},{2,6},{4,0},{6,2},{8,12},{10,14},{12,8},{14,10},{16,20},{18,... | collective-permute-start | bytes 4128776 | tf_op jit(solution)/shard_map/ppermute | solution.py:199
  409.7 25.4 %collective-permute-start.14 = (bf16[336,512]{1,0:T(8,128)(2,1)}, bf16[336,512]{1,0:T(8,128)(2,1)S(1)}, u32[]{:S(2)}, u32[]{:S(2)}) collective-permute-start(bf16[336,512]{1,0:T(8,128)(2,1)} %get-tuple-element.89), channel_id=1, source_target_pairs={{0,8},{2,10},{4,12},{6,14},{8,16},{10,18},{12,20},{14,22},{16,24},... | collective-permute-start | bytes 1032200 | tf_op jit(solution)/shard_map/ppermute | solution.py:212
  411.7 42.0 %collective-permute-start.15 = (bf16[336,512]{1,0:T(8,128)(2,1)}, bf16[336,512]{1,0:T(8,128)(2,1)S(1)}, u32[]{:S(2)}, u32[]{:S(2)}) collective-permute-start(bf16[336,512]{1,0:T(8,128)(2,1)} %get-tuple-element.88), channel_id=1, source_target_pairs={{0,16},{2,18},{4,20},{6,22},{8,24},{10,26},{12,28},{14,30},{16,0},... | collective-permute-start | bytes 1032200 | tf_op jit(solution)/shard_map/ppermute | solution.py:212
  413.5 43.5 %collective-permute-start.16 = (bf16[336,512]{1,0:T(8,128)(2,1)}, bf16[336,512]{1,0:T(8,128)(2,1)S(1)}, u32[]{:S(2)}, u32[]{:S(2)}) collective-permute-start(bf16[336,512]{1,0:T(8,128)(2,1)} %get-tuple-element.87), channel_id=1, source_target_pairs={{0,24},{2,26},{4,28},{6,30},{8,0},{10,2},{12,4},{14,6},{16,8},{18,... | collective-permute-start | bytes 1032200 | tf_op jit(solution)/shard_map/ppermute | solution.py:212
  413.7 101.6 %collective-permute-start.18 = (bf16[256,5376]{1,0:T(8,128)(2,1)}, bf16[256,5376]{1,0:T(8,128)(2,1)}, u32[]{:S(2)}, u32[]{:S(2)}) collective-permute-start(bf16[256,5376]{1,0:T(8,128)(2,1)} %fusion), channel_id=1, source_target_pairs={{0,1},{1,0},{2,3},{3,2},{4,5},{5,4},{6,7},{7,6},{8,9},{9,8},{10,11... | collective-permute-start | bytes 8257544 | tf_op jit(solution)/shard_map/ppermute | solution.py:342
  435.1 40.6 %collective-permute-start.23 = (bf16[336,512]{1,0:T(8,128)(2,1)S(1)}, bf16[336,512]{1,0:T(8,128)(2,1)S(1)}, u32[]{:S(2)}, u32[]{:S(2)}) collective-permute-start(bf16[336,512]{1,0:T(8,128)(2,1)S(1)} %get-tuple-element.81), channel_id=1, source_target_pairs={{0,8},{2,10},{4,12},{6,14},{8,16},{10,18},{12,20},{14,22},{16,24},... | collective-permute-start | bytes 1032200 | tf_op jit(solution)/shard_map/ppermute | solution.py:212
  453.7 24.6 %collective-permute-start.24 = (bf16[336,512]{1,0:T(8,128)(2,1)S(1)}, bf16[336,512]{1,0:T(8,128)(2,1)S(1)}, u32[]{:S(2)}, u32[]{:S(2)}) collective-permute-start(bf16[336,512]{1,0:T(8,128)(2,1)S(1)} %get-tuple-element.80), channel_id=1, source_target_pairs={{0,16},{2,18},{4,20},{6,22},{8,24},{10,26},{12,28},{14,30},{16,0},... | collective-permute-start | bytes 1032200 | tf_op jit(solution)/shard_map/ppermute | solution.py:212
  457.0 33.6 %collective-permute-start.25 = (bf16[336,512]{1,0:T(8,128)(2,1)}, bf16[336,512]{1,0:T(8,128)(2,1)}, u32[]{:S(2)}, u32[]{:S(2)}) collective-permute-start(bf16[336,512]{1,0:T(8,128)(2,1)} %get-tuple-element.79), channel_id=1, source_target_pairs={{0,24},{2,26},{4,28},{6,30},{8,0},{10,2},{12,4},{14,6},{16,8},{18,... | collective-permute-start | bytes 1032200 | tf_op jit(solution)/shard_map/ppermute | solution.py:212
  460.5 33.8 %collective-permute-start.26 = (bf16[336,512]{1,0:T(8,128)(2,1)}, bf16[336,512]{1,0:T(8,128)(2,1)}, u32[]{:S(2)}, u32[]{:S(2)}) collective-permute-start(bf16[336,512]{1,0:T(8,128)(2,1)} %get-tuple-element.77), channel_id=1, source_target_pairs={{0,8},{2,10},{4,12},{6,14},{8,16},{10,18},{12,20},{14,22},{16,24},... | collective-permute-start | bytes 1032200 | tf_op jit(solution)/shard_map/ppermute | solution.py:212
  476.4 22.8 %collective-permute-start.27 = (bf16[336,512]{1,0:T(8,128)(2,1)}, bf16[336,512]{1,0:T(8,128)(2,1)}, u32[]{:S(2)}, u32[]{:S(2)}) collective-permute-start(bf16[336,512]{1,0:T(8,128)(2,1)} %get-tuple-element.76), channel_id=1, source_target_pairs={{0,16},{2,18},{4,20},{6,22},{8,24},{10,26},{12,28},{14,30},{16,0},... | collective-permute-start | bytes 1032200 | tf_op jit(solution)/shard_map/ppermute | solution.py:212
  (47 other events, 503.0 us)
Sparse Core Ops, SparseCore 0:
  11.2 91.1 all-gather.2
  104.7 116.5 all-gather.4

commit v4 on v2

--- a/solution.py
+++ b/solution.py
@@ -122,34 +122,33 @@
         ref[:, d:] = acc[low : low + rows, d:].astype(jnp.bfloat16)
 
 
-def group_attention(qkv, kv_list, grad_out, key_start):
+def group_attention(qkv, kv_list, grad_out, key_start, place, grad_place):
     rows = qkv.shape[0]
     halo_span = len(kv_list) - 1
     d = HEAD_DIM
     q_cols = Q_PER_KV * d
-    groups = grad_out.shape[1] // q_cols
     ext = (halo_span + 1) * rows
     window = ATTEND_SPAN + TILE
-    elems = groups * Q_PER_KV * rows * window
-
-    def block(cols):
-        return pl.BlockSpec((rows, cols), lambda g: (0, g))
+    elems = Q_PER_KV * rows * window
+
+    def block(cols, at=0):
+        return pl.BlockSpec((rows, cols), lambda g: (0, at))
 
     def result(cols, kind):
-        return jax.ShapeDtypeStruct((rows, groups * cols), kind)
+        return jax.ShapeDtypeStruct((rows, cols), kind)
 
     return pl.pallas_call(
         functools.partial(attention_kernel, halo_span),
-        grid=(groups,),
+        grid=(1,),
         out_shape=(
             result(q_cols, jnp.bfloat16),
             result(q_cols, jnp.bfloat16),
             result(2 * d, jnp.float32),
         )
         + (result(2 * d, jnp.bfloat16),) * halo_span,
-        in_specs=[pl.BlockSpec(memory_space=pltpu.SMEM), block(q_cols + 2 * d)]
-        + [block(2 * d)] * (halo_span + 1)
-        + [block(q_cols)],
+        in_specs=[pl.BlockSpec(memory_space=pltpu.SMEM), block(q_cols + 2 * d, place)]
+        + [block(2 * d, place)] * (halo_span + 1)
+        + [block(q_cols, grad_place)],
         out_specs=(block(q_cols), block(q_cols), block(2 * d)) + (block(2 * d),) * halo_span,
         scratch_shapes=[
             pltpu.VMEM((ext, 2 * d), jnp.bfloat16),
@@ -159,7 +158,7 @@
         ],
         cost_estimate=pl.CostEstimate(
             flops=10 * elems * d,
-            bytes_accessed=groups * 6 * rows * 1024,
+            bytes_accessed=6 * rows * 1024,
             transcendentals=elems,
         ),
         compiler_params=pltpu.CompilerParams(vmem_limit_bytes=32 * 1024 * 1024),
@@ -182,7 +181,11 @@
     return other_core, pick(1 - mid, core), pick(mid, core)
 
 
-def reduce_rows(blocks, grad_qkv):
+def after(value, *earlier):
+    return lax.optimization_barrier((value, *earlier))[0]
+
+
+def reduce_rows(blocks, grad_qkv, earlier):
     other_core, other_chip, here = blocks
     seq_size = lax.axis_size("seq")
     outer_pos = lax.axis_index("seq") // 4
@@ -193,6 +196,7 @@
     got = lax.ppermute(sent, "seq", [(i, i ^ 1) for i in devices])
     sent = (dot_nn(other_chip, grad_qkv) + got[:half].astype(jnp.float32)).astype(jnp.bfloat16)
     got_chip = lax.ppermute(sent, "seq", [(i, i ^ 2) for i in devices])
+    got_chip = after(got_chip, *earlier)
     total = (
         dot_nn(here, grad_qkv) + got[half:].astype(jnp.float32) + got_chip.astype(jnp.float32)
     ).astype(jnp.bfloat16)
@@ -206,7 +210,7 @@
         route = [(i, (i + 4 * step) % seq_size) for i in devices]
         got = lax.ppermute(part((outer_pos + step) % outer), "seq", route)
         parts.append(got)
-    return total, parts
+    return sent, total, parts
 
 
 def adam_kernel(part_count, flag_ref, scale_ref, *refs):
@@ -271,12 +275,13 @@
     grad_out = (cotangent.astype(jnp.float32) * scale_power).astype(jnp.bfloat16)
 
     master16 = qkv_master.astype(jnp.bfloat16).reshape(own_rows, kv_groups * group_cols)
+    pair = 2 if kv_groups % 2 == 0 else 1
+    pair_cols = pair * group_cols
     weights = lax.all_gather(master16, "seq", axis=0, tiled=True)
     blocks = row_blocks(normed, own_rows)
-    pair = 2 if kv_groups % 2 == 0 else 1
-    outs, grads, sums = [], [], []
+    forward = []
     for low in range(0, kv_groups, pair):
-        qkv = dot_nn(normed, weights[:, low * group_cols : (low + pair) * group_cols])
+        qkv = dot_nn(normed, weights[:, low * group_cols : low * group_cols + pair_cols])
         kv, k_saved = [], []
         for g in range(pair):
             at = g * group_cols + q_cols
@@ -286,36 +291,47 @@
             kv += [k_unit.astype(jnp.bfloat16), qkv[:, at + d : at + 2 * d].astype(jnp.bfloat16)]
         kv = jnp.concatenate(kv, 1)
         kv_list = [shifted(kv, "seq", s) for s in range(halo_span, 0, -1)] + [kv]
-        out, gq, own, *backs = group_attention(
-            qkv, kv_list, grad_out[:, low * q_cols : (low + pair) * q_cols], key_start
-        )
+        forward.append((qkv, kv_list, k_saved))
+    outs, grads, sums, all_sent = [], [], [], []
+    waiting = []
+
+    def finish(gq, own, far_backs, k_raw, k_factor):
+        for back in far_backs:
+            back = after(back, outs[-1], *all_sent)
+            own = own + back.astype(jnp.float32)
+        gk = norm_back(k_raw, k_factor, own[:, :d])
+        grad_qkv = jnp.concatenate(
+            [gq, gk.astype(jnp.bfloat16), own[:, d:].astype(jnp.bfloat16)], 1
+        )
+        grad_qkv = lax.optimization_barrier(grad_qkv)
+        grads.append(grad_qkv)
+        earlier = sums[-2] if len(sums) >= 2 else ()
+        sent, _, parts = reduce_rows(blocks, grad_qkv, earlier)
+        all_sent.append(sent)
+        sums.append(parts)
+
+    for g in range(kv_groups):
+        qkv, kv_list, k_saved = forward[g // pair]
+        if len(waiting) == 3:
+            finish(*waiting.pop(0))
+        start = after(key_start, *(all_sent if all_sent else [x for f in forward for x in f[1]]))
+        out, gq, own, *backs = group_attention(qkv, kv_list, grad_out, start, g % pair, g)
         outs.append(out)
-        for s in range(1, halo_span + 1):
-            own = own + shifted(backs[s - 1], "seq", -s).astype(jnp.float32)
-        for g in range(pair):
-            at = g * 2 * d
-            gk = norm_back(*k_saved[g], own[:, at : at + d])
-            grad_qkv = jnp.concatenate(
-                [
-                    gq[:, g * q_cols : (g + 1) * q_cols],
-                    gk.astype(jnp.bfloat16),
-                    own[:, at + d : at + 2 * d].astype(jnp.bfloat16),
-                ],
-                1,
-            )
-            grad_qkv = lax.optimization_barrier(grad_qkv)
-            grads.append(grad_qkv)
-            total, parts = reduce_rows(blocks, grad_qkv)
-            sums.append(parts)
+        far_backs = [shifted(backs[s - 1], "seq", -s) for s in range(1, halo_span + 1)]
+        waiting.append((gq, own, far_backs, *k_saved[g % pair]))
+    while waiting:
+        finish(*waiting.pop(0))
     grad_qkv = jnp.concatenate(grads, 1)
+
+    def token_terms(rows_at, *earlier):
+        rows = lax.dynamic_slice_in_dim(grad_qkv, rows_at, part_rows, 0)
+        return dot_nt(after(rows, *earlier), weights)
+
     if head_count == 2:
-        peer_rows = lax.dynamic_slice_in_dim(grad_qkv, (1 - head_pos) * part_rows, part_rows, 0)
-        far_part = lax.ppermute(
-            dot_nt(peer_rows, weights).astype(jnp.bfloat16), "head", [(0, 1), (1, 0)]
-        )
-        far_part, _ = lax.optimization_barrier((far_part, total))
-        mine = lax.dynamic_slice_in_dim(grad_qkv, head_pos * part_rows, part_rows, 0)
-        d_tokens = dot_nt(mine, weights) + far_part.astype(jnp.float32)
+        peer_terms = token_terms((1 - head_pos) * part_rows, *all_sent).astype(jnp.bfloat16)
+        far_part = lax.ppermute(peer_terms, "head", [(0, 1), (1, 0)])
+        d_tokens = lax.optimization_barrier(token_terms(head_pos * part_rows, peer_terms))
+        d_tokens = d_tokens + far_part.astype(jnp.float32)
     else:
         d_tokens = lax.psum_scatter(
             dot_nt(grad_qkv, weights), "head", scatter_dimension=0, tiled=True

time: 521 us -> 487 us (0.935)
  the two profiles are of different devices: /device:TPU:8 before, /device:TPU:0 now
where the time goes in v4:
time: 487 us; the launch traced here: 482 us
  waiting for transfers between devices  203 us (42%)
  starting transfers between devices  85.8 us (18%)
  matrix products  67.4 us (14%)
  Pallas kernels  58.1 us (12%)
  local copies, waits for them, and re-layouts  32.7 us (7%)
  other arithmetic  19 us (4%)
  between operations  15.9 us (3%)
    all_gather x1, waiting for transfers between devices, per_device(): weights = lax.all_gather(master16, 'seq', axis=0, tiled=True)  117 us
    ppermute x4, waiting for transfers between devices, reduce_rows(): got_chip = lax.ppermute(sent, 'seq', [(i, i ^ 2) for i in devices])  48.9 us
    pallas_call x4, Pallas kernels, group_attention(): pl.pallas_call(functools.partial(attention_kernel, halo_span), grid=(1,),...  48.1 us
    ppermute x12, starting transfers between devices, reduce_rows(): got = lax.ppermute(part((outer_pos + step) % outer), 'seq', route)  46.8 us
    dot_general x14, matrix products, dot_nn(): return jnp.dot(a, b, preferred_element_type=jnp.float32)  43 us
    unnamed x116, local copies, waits for them, and re-layouts  26.3 us
    ppermute x12, waiting for transfers between devices, reduce_rows(): got = lax.ppermute(part((outer_pos + step) % outer), 'seq', route)  25.6 us
    dot_general x2, matrix products, dot_nt(): lax.dot_general(a, b, (((1,), (1,)), ((), ())), preferred_element_type=jn...  24.4 us
  transfers between devices with their start and end apart: 34, of which 12 were waited for; matrix products, arithmetic and copies ran while one was open for 16% of the time, Pallas kernels for 10%

profile of v4, /device:TPU:0, one launch (start us, length us, event | category | flops | bytes accessed | tf_op | source)
XLA Modules:
  0.0 481.5 jit_solution(14500766604271019126)
XLA Ops:
  10.9 116.6 %all-gather.2.cloned.1.call-done = bf16[5376,2048]{1,0:T(8,128)(2,1)} async-done(((bf16[336,2048]{1,0:T(8,128)(2,1)}), bf16[5376,2048]{1,0:T(8,128)(2,1)}) %all-gather.2.cloned.1.call-update) | async-done | bytes 22020112 | tf_op jit(solution)/shard_map/all_gather | solution.py:280
  127.6 10.4 %fusion.7 = (bf16[512,1024]{1,0:T(8,128)(2,1)S(1)}, f32[512,1024]{1,0:T(8,128)S(1)}) fusion(bf16[512,5376]{1,0:T(8,128)(2,1)} %param.7, bf16[5376,2048]{1,0:T(8,128)(2,1)} %all-gather.2.cloned.1.call-done), kind=kOutput, calls=%fused_computation.85 | convolution fusion | flops 5637668864 | bytes 19660800 | tf_op jit(solution)/shard_map/dot_general | solution.py:49
  144.8 8.0 %fusion.6 = (bf16[512,1024]{1,0:T(8,128)(2,1)S(1)}, f32[512,1024]{1,0:T(8,128)S(1)}) fusion(bf16[512,5376]{1,0:T(8,128)(2,1)} %param.7, bf16[5376,2048]{1,0:T(8,128)(2,1)S(1)} %copy-done.54), kind=kOutput, calls=%fused_computation.84 | convolution fusion | flops 5637668864 | bytes 19660800 | tf_op jit(solution)/shard_map/dot_general | solution.py:49
  154.7 4.0 collective-permute-start.1
  161.6 8.2 %copy.12 = bf16[512,5376]{0,1:T(8,128)(2,1)} copy(bf16[512,5376]{1,0:T(8,128)(2,1)} %param.7) | data formatting | bytes 11010048 | tf_op args[0]
  174.2 11.9 %shard_map.110 = (bf16[512,256]{1,0:T(8,128)(2,1)S(1)}, bf16[512,256]{1,0:T(8,128)(2,1)S(1)}, f32[512,256]{1,0:T(8,128)S(1)}, bf16[512,256]{1,0:T(8,128)(2,1)S(1)}, bf16[512,256]{1,0:T(8,128)(2,1)S(1)}) custom-call(s32[1]{0:T(128)} %bitcast.start_ref, f32[512,1024]{1,0:T(8,128)S(1)} %copy-done.4, bf16[512,512]{1,0:T(8,128)(2,1)} %collective-permute-done.refs_0_, ...), custom_call_target="tpu_custom_call" | custom-call | flops 1509949440 | bytes 3145728 | tf_op jit(solution)/shard_map/pallas_call | solution.py:140
  191.2 12.4 %shard_map.112 = (bf16[512,256]{1,0:T(8,128)(2,1)S(1)}, bf16[512,256]{1,0:T(8,128)(2,1)S(1)}, f32[512,256]{1,0:T(8,128)S(1)}, bf16[512,256]{1,0:T(8,128)(2,1)S(1)}, bf16[512,256]{1,0:T(8,128)(2,1)S(1)}) custom-call(s32[1]{0:T(128)} %bitcast.start_ref, f32[512,1024]{1,0:T(8,128)S(1)} %get-tuple-element.116.qkv_ref, ...), custom_call_target="tpu_custom_call" | custom-call | flops 1509949440 | bytes 3145728 | tf_op jit(solution)/shard_map/pallas_call | solution.py:140
  205.9 4.0 collective-permute-start.6
  209.9 12.1 %shard_map.111 = (bf16[512,256]{1,0:T(8,128)(2,1)S(1)}, bf16[512,256]{1,0:T(8,128)(2,1)S(1)}, f32[512,256]{1,0:T(8,128)S(1)}, bf16[512,256]{1,0:T(8,128)(2,1)S(1)}, bf16[512,256]{1,0:T(8,128)(2,1)S(1)}) custom-call(s32[1]{0:T(128)} %bitcast.start_ref, f32[512,1024]{1,0:T(8,128)S(1)} %copy-done.5, bf16[512,512]{1,0:T(8,128)(2,1)} %collective-permute-done.refs_0_, ...), custom_call_target="tpu_custom_call" | custom-call | flops 1509949440 | bytes 3145728 | tf_op jit(solution)/shard_map/pallas_call | solution.py:140
  227.4 11.8 %shard_map.113 = (bf16[512,256]{1,0:T(8,128)(2,1)S(1)}, bf16[512,256]{1,0:T(8,128)(2,1)S(1)}, f32[512,256]{1,0:T(8,128)S(1)}, bf16[512,256]{1,0:T(8,128)(2,1)S(1)}, bf16[512,256]{1,0:T(8,128)(2,1)S(1)}) custom-call(s32[1]{0:T(128)} %bitcast.start_ref, f32[512,1024]{1,0:T(8,128)S(1)} %get-tuple-element.116.qkv_ref, ...), custom_call_target="tpu_custom_call" | custom-call | flops 1509949440 | bytes 3145728 | tf_op jit(solution)/shard_map/pallas_call | solution.py:140
  249.3 8.7 %collective-permute-done.11 = bf16[512,256]{1,0:T(8,128)(2,1)S(1)} collective-permute-done((bf16[512,256]{1,0:T(8,128)(2,1)S(1)}, bf16[512,256]{1,0:T(8,128)(2,1)S(1)}, u32[]{:S(2)}, u32[]{:S(2)}) %collective-permute-start.11) | collective-permute-done | bytes 262176 | tf_op jit(solution)/shard_map/ppermute | solution.py:31
  271.7 31.5 %collective-permute-done.17 = bf16[1344,512]{1,0:T(8,128)(2,1)} collective-permute-done((bf16[1344,512]{1,0:T(8,128)(2,1)}, bf16[1344,512]{1,0:T(8,128)(2,1)}, u32[]{:S(2)}, u32[]{:S(2)}) %collective-permute-start.17) | collective-permute-done | bytes 1376288 | tf_op jit(solution)/shard_map/ppermute | solution.py:198
  313.5 5.4 %collective-permute-start.20 = (bf16[336,512]{1,0:T(8,128)(2,1)S(1)}, bf16[336,512]{1,0:T(8,128)(2,1)S(1)}, u32[]{:S(2)}, u32[]{:S(2)}) collective-permute-start(bf16[336,512]{1,0:T(8,128)(2,1)S(1)} %get-tuple-element.105), channel_id=1, source_target_pairs={{0,24},{2,26},{4,28},{6,30},{8,0},{10,2},{12,4},{14,6},{16,8},{18,... | collective-permute-start | bytes 1032200 | tf_op jit(solution)/shard_map/ppermute | solution.py:211
  324.0 11.8 %collective-permute-done.21 = bf16[1344,512]{1,0:T(8,128)(2,1)S(1)} collective-permute-done((bf16[1344,512]{1,0:T(8,128)(2,1)S(1)}, bf16[1344,512]{1,0:T(8,128)(2,1)S(1)}, u32[]{:S(2)}, u32[]{:S(2)}) %collective-permute-start.21) | collective-permute-done | bytes 1376288 | tf_op jit(solution)/shard_map/ppermute | solution.py:198
  343.4 3.7 collective-permute-start.24
  350.6 14.8 %collective-permute-start.22 = (bf16[336,512]{1,0:T(8,128)(2,1)}, bf16[336,512]{1,0:T(8,128)(2,1)S(1)}, u32[]{:S(2)}, u32[]{:S(2)}) collective-permute-start(bf16[336,512]{1,0:T(8,128)(2,1)} %get-tuple-element.103), channel_id=1, source_target_pairs={{0,8},{2,10},{4,12},{6,14},{8,16},{10,18},{12,20},{14,22},{16,24},... | collective-permute-start | bytes 1032200 | tf_op jit(solution)/shard_map/ppermute | solution.py:211
  370.9 11.9 %convolution_convert_fusion = bf16[256,5376]{1,0:T(8,128)(2,1)} fusion(bf16[256,2048]{1,0:T(8,128)(2,1)} %get-tuple-element.72, bf16[5376,2048]{1,0:T(8,128)(2,1)} %all-gather.2.cloned.1.call-done), kind=kOutput, calls=%fused_computation.4 | convolution fusion | flops 5638520832 | bytes 25821184 | tf_op jit(solution)/shard_map/dot_general | solution.py:45
  389.9 4.2 collective-permute-start.27
  396.1 4.0 collective-permute-done.29
  404.8 11.2 %collective-permute-start.31 = (bf16[336,512]{1,0:T(8,128)(2,1)}, bf16[336,512]{1,0:T(8,128)(2,1)}, u32[]{:S(2)}, u32[]{:S(2)}) collective-permute-start(bf16[336,512]{1,0:T(8,128)(2,1)} %get-tuple-element.94), channel_id=1, source_target_pairs={{0,16},{2,18},{4,20},{6,22},{8,24},{10,26},{12,28},{14,30},{16,0},... | collective-permute-start | bytes 1032200 | tf_op jit(solution)/shard_map/ppermute | solution.py:211
  416.0 20.2 %collective-permute-done.27.refs_10_ = bf16[336,512]{1,0:T(8,128)(2,1)S(1)} collective-permute-done((bf16[336,512]{1,0:T(8,128)(2,1)S(1)}, bf16[336,512]{1,0:T(8,128)(2,1)S(1)}, u32[]{:S(2)}, u32[]{:S(2)}) %collective-permute-start.27) | collective-permute-done | bytes 344096 | tf_op jit(solution)/shard_map/ppermute | solution.py:211
  436.9 12.5 %fusion.8 = f32[256,5376]{1,0:T(8,128)} fusion(bf16[256,2048]{1,0:T(8,128)(2,1)} %get-tuple-element.73, bf16[5376,2048]{1,0:T(8,128)(2,1)} %all-gather.2.cloned.1.call-done), kind=kOutput, calls=%fused_computation.86 | convolution fusion | flops 5637144576 | bytes 28573696 | tf_op jit(solution)/shard_map/dot_general | solution.py:45
  460.7 9.9 %shard_map.114 = (f32[336,4,512]{2,1,0:T(4,128)}, f32[336,4,512]{2,1,0:T(4,128)}, f32[336,4,512]{2,1,0:T(4,128)}) custom-call(s32[4]{0:T(128)S(1)} %dynamic_slice.81.flag_ref, f32[1]{0:T(128)} %bitcast.8.scale_ref, bf16[336,512]{1,0:T(8,128)(2,1)S(1)} %get-tuple-element.108.refs_0_, bf16[336,512]{1,0:T(8,128)(2,1)S(1)} %copy-done.7, ...), custom_call_target="tpu_custom_call" | custom-call | flops 13762560 | bytes 22020096 | tf_op jit(solution)/shard_map/pallas_call | solution.py:250
  470.7 3.8 add_convert_fusion
  (232 shorter events, 112.8 us)
Async XLA Ops:
  7.2 120.4 %all-gather.2.cloned.1.call-start = ((), (), s32[]{:S(2)}) async-start(), calls=%async_computation | async-start | bytes 23396352 | tf_op jit(solution)/shard_map/all_gather | solution.py:280
  138.5 33.4 %collective-permute-start.3 = (bf16[512,512]{1,0:T(8,128)(2,1)S(1)}, bf16[512,512]{1,0:T(8,128)(2,1)}, u32[]{:S(2)}, u32[]{:S(2)}) collective-permute-start(bf16[512,512]{1,0:T(8,128)(2,1)S(1)} %pad_maximum_fusion.4.refs_2_), channel_id=1, source_target_pairs={{0,2},{2,4},{4,6},{6,8},{8,10},{10,12},{12,14},{14,16},{16,18},{18... | collective-permute-start | bytes 1572872 | tf_op jit(solution)/shard_map/ppermute | solution.py:31
  141.7 30.3 %collective-permute-start.2 = (bf16[512,512]{1,0:T(8,128)(2,1)S(1)}, bf16[512,512]{1,0:T(8,128)(2,1)}, u32[]{:S(2)}, u32[]{:S(2)}) collective-permute-start(bf16[512,512]{1,0:T(8,128)(2,1)S(1)} %pad_maximum_fusion.4.refs_2_), channel_id=1, source_target_pairs={{0,4},{2,6},{4,8},{6,10},{8,12},{10,14},{12,16},{14,18},{16,20},{1... | collective-permute-start | bytes 1572872 | tf_op jit(solution)/shard_map/ppermute | solution.py:31
  154.7 17.3 %collective-permute-start.1 = (bf16[512,512]{1,0:T(8,128)(2,1)S(1)}, bf16[512,512]{1,0:T(8,128)(2,1)}, u32[]{:S(2)}, u32[]{:S(2)}) collective-permute-start(bf16[512,512]{1,0:T(8,128)(2,1)S(1)} %pad_maximum_fusion.3.refs_2_), channel_id=1, source_target_pairs={{0,2},{2,4},{4,6},{6,8},{8,10},{10,12},{12,14},{14,16},{16,18},{18... | collective-permute-start | bytes 1572872 | tf_op jit(solution)/shard_map/ppermute | solution.py:31
  205.9 19.4 %collective-permute-start.6 = (bf16[2688,512]{1,0:T(8,128)(2,1)S(1)}, bf16[2688,512]{1,0:T(8,128)(2,1)S(1)}, u32[]{:S(2)}, u32[]{:S(2)}) collective-permute-start(bf16[2688,512]{1,0:T(8,128)(2,1)S(1)} %convolution_convert_fusion.4), channel_id=1, source_target_pairs={{0,2},{2,0},{4,6},{6,4},{8,10},{10,8},{12,14},{14,12},{16,18},{18,... | collective-permute-start | bytes 8257544 | tf_op jit(solution)/shard_map/ppermute | solution.py:196
  261.7 44.0 %collective-permute-start.13 = (bf16[2688,512]{1,0:T(8,128)(2,1)}, bf16[2688,512]{1,0:T(8,128)(2,1)}, u32[]{:S(2)}, u32[]{:S(2)}) collective-permute-start(bf16[2688,512]{1,0:T(8,128)(2,1)} %convolution_convert_fusion.2), channel_id=1, source_target_pairs={{0,2},{2,0},{4,6},{6,4},{8,10},{10,8},{12,14},{14,12},{16,18},{18,... | collective-permute-start | bytes 8257544 | tf_op jit(solution)/shard_map/ppermute | solution.py:196
  261.7 41.5 %collective-permute-start.17 = (bf16[1344,512]{1,0:T(8,128)(2,1)}, bf16[1344,512]{1,0:T(8,128)(2,1)}, u32[]{:S(2)}, u32[]{:S(2)}) collective-permute-start(bf16[1344,512]{1,0:T(8,128)(2,1)} %add_convert_fusion.8), channel_id=1, source_target_pairs={{0,4},{2,6},{4,0},{6,2},{8,12},{10,14},{12,8},{14,10},{16,20},{18,... | collective-permute-start | bytes 4128776 | tf_op jit(solution)/shard_map/ppermute | solution.py:198
  266.9 41.0 %collective-permute-start.12 = (bf16[512,256]{1,0:T(8,128)(2,1)S(1)}, bf16[512,256]{1,0:T(8,128)(2,1)S(1)}, u32[]{:S(2)}, u32[]{:S(2)}) collective-permute-start(bf16[512,256]{1,0:T(8,128)(2,1)S(1)} %copy-done.27), channel_id=1, source_target_pairs={{2,0},{4,2},{6,4},{8,6},{10,8},{12,10},{14,12},{16,14},{18,16},{20... | collective-permute-start | bytes 786440 | tf_op jit(solution)/shard_map/ppermute | solution.py:31
  268.4 39.6 %collective-permute-start.14 = (bf16[512,256]{1,0:T(8,128)(2,1)S(1)}, bf16[512,256]{1,0:T(8,128)(2,1)S(1)}, u32[]{:S(2)}, u32[]{:S(2)}) collective-permute-start(bf16[512,256]{1,0:T(8,128)(2,1)S(1)} %copy-done.29), channel_id=1, source_target_pairs={{4,0},{6,2},{8,4},{10,6},{12,8},{14,10},{16,12},{18,14},{20,16},{2... | collective-permute-start | bytes 786440 | tf_op jit(solution)/shard_map/ppermute | solution.py:31
  303.2 32.6 %collective-permute-start.21 = (bf16[1344,512]{1,0:T(8,128)(2,1)S(1)}, bf16[1344,512]{1,0:T(8,128)(2,1)S(1)}, u32[]{:S(2)}, u32[]{:S(2)}) collective-permute-start(bf16[1344,512]{1,0:T(8,128)(2,1)S(1)} %copy-done.55), channel_id=1, source_target_pairs={{0,4},{2,6},{4,0},{6,2},{8,12},{10,14},{12,8},{14,10},{16,20},{18,... | collective-permute-start | bytes 4128776 | tf_op jit(solution)/shard_map/ppermute | solution.py:198
  311.3 55.7 %collective-permute-start.15 = (bf16[2688,512]{1,0:T(8,128)(2,1)S(1)}, bf16[2688,512]{1,0:T(8,128)(2,1)S(1)}, u32[]{:S(2)}, u32[]{:S(2)}) collective-permute-start(bf16[2688,512]{1,0:T(8,128)(2,1)S(1)} %convolution_convert_fusion.1), channel_id=1, source_target_pairs={{0,2},{2,0},{4,6},{6,4},{8,10},{10,8},{12,14},{14,12},{16,18},{18,... | collective-permute-start | bytes 8257544 | tf_op jit(solution)/shard_map/ppermute | solution.py:196
  313.5 29.9 %collective-permute-start.20 = (bf16[336,512]{1,0:T(8,128)(2,1)S(1)}, bf16[336,512]{1,0:T(8,128)(2,1)S(1)}, u32[]{:S(2)}, u32[]{:S(2)}) collective-permute-start(bf16[336,512]{1,0:T(8,128)(2,1)S(1)} %get-tuple-element.105), channel_id=1, source_target_pairs={{0,24},{2,26},{4,28},{6,30},{8,0},{10,2},{12,4},{14,6},{16,8},{18,... | collective-permute-start | bytes 1032200 | tf_op jit(solution)/shard_map/ppermute | solution.py:211
  318.9 31.7 %collective-permute-start.19 = (bf16[336,512]{1,0:T(8,128)(2,1)S(1)}, bf16[336,512]{1,0:T(8,128)(2,1)S(1)}, u32[]{:S(2)}, u32[]{:S(2)}) collective-permute-start(bf16[336,512]{1,0:T(8,128)(2,1)S(1)} %get-tuple-element.106), channel_id=1, source_target_pairs={{0,16},{2,18},{4,20},{6,22},{8,24},{10,26},{12,28},{14,30},{16,0},... | collective-permute-start | bytes 1032200 | tf_op jit(solution)/shard_map/ppermute | solution.py:211
  319.6 31.0 %collective-permute-start.18 = (bf16[336,512]{1,0:T(8,128)(2,1)S(1)}, bf16[336,512]{1,0:T(8,128)(2,1)S(1)}, u32[]{:S(2)}, u32[]{:S(2)}) collective-permute-start(bf16[336,512]{1,0:T(8,128)(2,1)S(1)} %get-tuple-element.107), channel_id=1, source_target_pairs={{0,8},{2,10},{4,12},{6,14},{8,16},{10,18},{12,20},{14,22},{16,24},... | collective-permute-start | bytes 1032200 | tf_op jit(solution)/shard_map/ppermute | solution.py:211
  335.7 31.2 %collective-permute-start.25 = (bf16[1344,512]{1,0:T(8,128)(2,1)S(1)}, bf16[1344,512]{1,0:T(8,128)(2,1)S(1)}, u32[]{:S(2)}, u32[]{:S(2)}) collective-permute-start(bf16[1344,512]{1,0:T(8,128)(2,1)S(1)} %add_convert_fusion.6), channel_id=1, source_target_pairs={{0,4},{2,6},{4,0},{6,2},{8,12},{10,14},{12,8},{14,10},{16,20},{18,... | collective-permute-start | bytes 4128776 | tf_op jit(solution)/shard_map/ppermute | solution.py:198
  343.4 44.6 %collective-permute-start.24 = (bf16[336,512]{1,0:T(8,128)(2,1)}, bf16[336,512]{1,0:T(8,128)(2,1)S(1)}, u32[]{:S(2)}, u32[]{:S(2)}) collective-permute-start(bf16[336,512]{1,0:T(8,128)(2,1)} %get-tuple-element.101), channel_id=1, source_target_pairs={{0,24},{2,26},{4,28},{6,30},{8,0},{10,2},{12,4},{14,6},{16,8},{18,... | collective-permute-start | bytes 1032200 | tf_op jit(solution)/shard_map/ppermute | solution.py:211
  350.6 39.3 %collective-permute-start.23 = (bf16[336,512]{1,0:T(8,128)(2,1)}, bf16[336,512]{1,0:T(8,128)(2,1)S(1)}, u32[]{:S(2)}, u32[]{:S(2)}) collective-permute-start(bf16[336,512]{1,0:T(8,128)(2,1)} %get-tuple-element.102), channel_id=1, source_target_pairs={{0,16},{2,18},{4,20},{6,22},{8,24},{10,26},{12,28},{14,30},{16,0},... | collective-permute-start | bytes 1032200 | tf_op jit(solution)/shard_map/ppermute | solution.py:211
  350.6 43.5 %collective-permute-start.22 = (bf16[336,512]{1,0:T(8,128)(2,1)}, bf16[336,512]{1,0:T(8,128)(2,1)S(1)}, u32[]{:S(2)}, u32[]{:S(2)}) collective-permute-start(bf16[336,512]{1,0:T(8,128)(2,1)} %get-tuple-element.103), channel_id=1, source_target_pairs={{0,8},{2,10},{4,12},{6,14},{8,16},{10,18},{12,20},{14,22},{16,24},... | collective-permute-start | bytes 1032200 | tf_op jit(solution)/shard_map/ppermute | solution.py:211
  369.4 30.6 %collective-permute-start.29 = (bf16[1344,512]{1,0:T(8,128)(2,1)}, bf16[1344,512]{1,0:T(8,128)(2,1)}, u32[]{:S(2)}, u32[]{:S(2)}) collective-permute-start(bf16[1344,512]{1,0:T(8,128)(2,1)} %add_convert_fusion.5), channel_id=1, source_target_pairs={{0,4},{2,6},{4,0},{6,2},{8,12},{10,14},{12,8},{14,10},{16,20},{18,... | collective-permute-start | bytes 4128776 | tf_op jit(solution)/shard_map/ppermute | solution.py:198
  382.8 87.9 %collective-permute-start.16 = (bf16[256,5376]{1,0:T(8,128)(2,1)}, bf16[256,5376]{1,0:T(8,128)(2,1)}, u32[]{:S(2)}, u32[]{:S(2)}) collective-permute-start(bf16[256,5376]{1,0:T(8,128)(2,1)} %convolution_convert_fusion), channel_id=1, source_target_pairs={{0,1},{1,0},{2,3},{3,2},{4,5},{5,4},{6,7},{7,6},{8,9},{9,8},{10,11... | collective-permute-start | bytes 8257544 | tf_op jit(solution)/shard_map/ppermute | solution.py:332
  389.9 46.3 %collective-permute-start.27 = (bf16[336,512]{1,0:T(8,128)(2,1)S(1)}, bf16[336,512]{1,0:T(8,128)(2,1)S(1)}, u32[]{:S(2)}, u32[]{:S(2)}) collective-permute-start(bf16[336,512]{1,0:T(8,128)(2,1)S(1)} %get-tuple-element.98), channel_id=1, source_target_pairs={{0,16},{2,18},{4,20},{6,22},{8,24},{10,26},{12,28},{14,30},{16,0},... | collective-permute-start | bytes 1032200 | tf_op jit(solution)/shard_map/ppermute | solution.py:211
  394.1 55.3 %collective-permute-start.26 = (bf16[336,512]{1,0:T(8,128)(2,1)}, bf16[336,512]{1,0:T(8,128)(2,1)}, u32[]{:S(2)}, u32[]{:S(2)}) collective-permute-start(bf16[336,512]{1,0:T(8,128)(2,1)} %get-tuple-element.99), channel_id=1, source_target_pairs={{0,8},{2,10},{4,12},{6,14},{8,16},{10,18},{12,20},{14,22},{16,24},... | collective-permute-start | bytes 1032200 | tf_op jit(solution)/shard_map/ppermute | solution.py:211
  403.0 46.4 %collective-permute-start.32 = (bf16[336,512]{1,0:T(8,128)(2,1)}, bf16[336,512]{1,0:T(8,128)(2,1)}, u32[]{:S(2)}, u32[]{:S(2)}) collective-permute-start(bf16[336,512]{1,0:T(8,128)(2,1)} %get-tuple-element.93), channel_id=1, source_target_pairs={{0,24},{2,26},{4,28},{6,30},{8,0},{10,2},{12,4},{14,6},{16,8},{18,... | collective-permute-start | bytes 1032200 | tf_op jit(solution)/shard_map/ppermute | solution.py:211
  404.8 46.5 %collective-permute-start.31 = (bf16[336,512]{1,0:T(8,128)(2,1)}, bf16[336,512]{1,0:T(8,128)(2,1)}, u32[]{:S(2)}, u32[]{:S(2)}) collective-permute-start(bf16[336,512]{1,0:T(8,128)(2,1)} %get-tuple-element.94), channel_id=1, source_target_pairs={{0,16},{2,18},{4,20},{6,22},{8,24},{10,26},{12,28},{14,30},{16,0},... | collective-permute-start | bytes 1032200 | tf_op jit(solution)/shard_map/ppermute | solution.py:211
  (67 other events, 773.0 us)
Sparse Core Ops, SparseCore 0:
  11.1 116.4 all-gather.1
